TPU v7x, 256 devices: a whole 4x4x8 slice. The times are simulated.
256 devices in a mesh: leaf: 64 (over z, x, core), blk: 4 (over y).
Axes of the slice: x: 4, y: 4, z: 8, core: 2. Of those that a mesh axis runs over, the one named last changes fastest.
Arguments:
- points: bfloat16 [64, 1024, 512], P(None, 'leaf', 'blk')
- charges: bfloat16 [16, 1024, 512], P(None, 'leaf', 'blk'), may hold values from -6 to 6
- leaf_interp: bfloat16 [1024, 256, 512], P('leaf'), may hold values from -0.25 to 0.25
- root_interp: bfloat16 [1024, 256, 256], P('leaf'), may hold values from -0.09375 to 0.09375
- skeleton_index: int32 [1024, 256], P('leaf'), may hold values from 0 to 511, as said below
- root_index: int32 [64, 256], P('leaf'), may hold values from 0 to 4095, as said below
- near_list: int32 [1024, 10], P('leaf'), may hold values from 0 to 1023, as said below
- far_list: int32 [1024, 32], P('leaf'), may hold values from 0 to 1023, as said below
- far_count: int32 [1024], P('leaf'), may hold values from 1 to 32, as said below
Outputs:
- potentials: float32 [16, 1024, 512], P(None, 'leaf', 'blk')
Inputs may be any that keep to these rules, and one draw needn't show every extreme that they name: `skeleton_index`: each row names 256 different points of its leaf. `root_index`: row o names 256 different skeleton points of owner o, numbered leaf by leaf with 256 to a leaf. `near_list`: row l names 10 different leaves, l among them, all in the window of 17 consecutive leaves that begins at max(0, min(l - 8, 1007)); both ends of that window are named. `far_list`: leaf l belongs to owner o = l // 16; its first far_count[l] entries are different leaves of the existing owners among o - 2, o - 1, o + 1, o + 2, and its later entries repeat l and are not used; over the used entries of all leaves of one owner, each of those owners has exactly 8 different leaves named. `far_count`: at most the number of leaves that the owner's far lists can name (32 for owners at distance 2 or more from both ends); the first leaf of every owner uses all of them; the mean load differs strongly from owner to owner.
All inputs are finite; a program needn't handle non-finite values.
Results may differ from a plain program's by a relative error of at most 0.0036.
Values may be sent and summed in bfloat16 or wider, within the bound.
A program may use at most 128 MiB of HBM per device.

v0:
```python
import jax
import jax.numpy as jnp
from jax import lax
from jax.sharding import PartitionSpec as P

HALO = 8
NEAR = 10
FAR = 32


neighbour_steps = (-2, -1, 1, 2)


def with_halo(block, sides, width):
    for axis, dim in sides:
        count = lax.axis_size(axis)
        forward = [(i, i + 1) for i in range(count - 1)]
        backward = [(target, source) for source, target in forward]
        low = lax.ppermute(
            lax.slice_in_dim(block, block.shape[dim] - width, None, axis=dim), axis, forward
        )
        high = lax.ppermute(lax.slice_in_dim(block, 0, width, axis=dim), axis, backward)
        block = jnp.concatenate([low, block, high], axis=dim)
    return block


def shifted(block, axis, distance):
    devices = range(lax.axis_size(axis))
    route = [(i - distance, i) for i in devices if i - distance in devices]
    return lax.ppermute(block, axis, route)


def kernel_block(sources, targets):
    inner_prod = lax.dot_general(
        sources, targets, (((0,), (0,)), ((), ())), preferred_element_type=jnp.float32
    )
    source_norm = jnp.sum(jnp.square(sources.astype(jnp.float32)), axis=0)
    target_norm = jnp.sum(jnp.square(targets.astype(jnp.float32)), axis=0)
    return jnp.exp(inner_prod - 0.5 * source_norm[:, None] - 0.5 * target_norm[None, :]).astype(
        jnp.bfloat16
    )


def one_hot_rows(indices, row_total):
    return (indices[..., None] == jnp.arange(row_total, dtype=jnp.int32)).astype(jnp.bfloat16)


def on_device(
    points,
    charges,
    leaf_interp,
    root_interp,
    skeleton_index,
    root_index,
    near_list,
    far_list,
    far_count,
):
    coord_count = points.shape[0]
    leaf_count = points.shape[1]
    block_points = points.shape[2]
    rhs_count = charges.shape[0]
    skeleton = leaf_interp.shape[1]
    leaf_width = leaf_interp.shape[2]
    block_count = lax.axis_size("blk")
    block_index = lax.axis_index("blk")
    owner_index = lax.axis_index("leaf")
    quarter = skeleton // block_count
    first_leaf = owner_index * leaf_count
    stacked = jnp.concatenate([points, charges], axis=0)
    gathered = lax.all_gather(stacked, "blk", axis=2, tiled=True)
    extended = with_halo(gathered, (("leaf", 1),), HALO)
    leaf_points = gathered[:coord_count]
    leaf_charges = gathered[coord_count:]
    skeleton_weights = jnp.einsum(
        "lsm,zlm->zls", leaf_interp, leaf_charges, preferred_element_type=jnp.float32
    ).astype(jnp.bfloat16)
    skeleton_pick = one_hot_rows(skeleton_index, leaf_width)
    skeleton_points = jnp.einsum(
        "dlm,lsm->dls", leaf_points, skeleton_pick, preferred_element_type=jnp.float32
    ).astype(jnp.bfloat16)
    skeleton_data = jnp.concatenate([skeleton_points, skeleton_weights], axis=0)
    root_weights = jnp.einsum(
        "lrs,zls->zr", root_interp, skeleton_weights, preferred_element_type=jnp.float32
    ).astype(jnp.bfloat16)
    root_pick = one_hot_rows(root_index[0], leaf_count * skeleton)
    root_points = jnp.einsum(
        "dc,rc->dr",
        skeleton_points.reshape(coord_count, leaf_count * skeleton),
        root_pick,
        preferred_element_type=jnp.float32,
    ).astype(jnp.bfloat16)
    root_data = jnp.concatenate([root_points, root_weights], axis=0)
    fetched = lax.all_gather(root_data, "leaf", axis=1, tiled=True)
    columns = fetched.shape[1]
    source_owner = jnp.arange(columns, dtype=jnp.int32) // skeleton
    distant = jnp.abs(source_owner - owner_index) > 2
    kernel = kernel_block(fetched[:coord_count], root_points)
    kernel = jnp.where(distant[:, None], kernel, jnp.zeros_like(kernel))
    root_field = jnp.dot(fetched[coord_count:], kernel, preferred_element_type=jnp.float32)
    root_field = root_field.astype(jnp.bfloat16)
    skeleton_targets = lax.dynamic_slice_in_dim(skeleton_points, block_index * quarter, quarter, 2)
    source_owner = far_list // leaf_count
    offset_of = source_owner - owner_index
    position = offset_of + 2 - (offset_of > 0).astype(jnp.int32)
    local_leaf = far_list - source_owner * leaf_count
    fetched_parts = []
    for offset in neighbour_steps:
        fetched_parts.append(shifted(skeleton_data, "leaf", -offset))
    sources_table = jnp.concatenate(fetched_parts, axis=1)
    table_row = position * leaf_count + local_leaf
    table_rows_total = sources_table.shape[1]
    table_row = jnp.clip(table_row, 0, table_rows_total - 1)
    source_width = sources_table.shape[2]
    slot_ids = jnp.arange(FAR, dtype=jnp.int32)
    far_pick = one_hot_rows(table_row, table_rows_total)
    far_sources_all = jnp.einsum(
        "crs,ljr->cljs", sources_table, far_pick, preferred_element_type=jnp.float32
    ).astype(jnp.bfloat16)

    def far_leaf(leaf_pos):
        picked = lax.dynamic_index_in_dim(far_sources_all, leaf_pos, 1, keepdims=False).reshape(
            sources_table.shape[0], FAR * source_width
        )
        target = lax.dynamic_index_in_dim(skeleton_targets, leaf_pos, 1, keepdims=False)
        kernel = kernel_block(picked[:coord_count], target)
        live_rows = jnp.repeat(slot_ids < far_count[leaf_pos], source_width)
        kernel = jnp.where(live_rows[:, None], kernel, jnp.zeros_like(kernel))
        return jnp.dot(picked[coord_count:], kernel, preferred_element_type=jnp.float32)

    far_field = lax.map(far_leaf, jnp.arange(leaf_count, dtype=jnp.int32))
    root_columns = lax.dynamic_slice_in_dim(root_interp, block_index * quarter, quarter, 2)
    lifted = jnp.einsum("lrs,zr->lzs", root_columns, root_field, preferred_element_type=jnp.float32)
    skeleton_field = (far_field + lifted).astype(jnp.bfloat16)
    interp_rows = lax.dynamic_slice_in_dim(leaf_interp, block_index * quarter, quarter, 1)
    partial_term = jnp.einsum(
        "lsm,lzs->mzl", interp_rows, skeleton_field, preferred_element_type=jnp.float32
    )
    spread = lax.psum_scatter(
        partial_term.reshape(block_points * lax.axis_size("blk"), rhs_count * leaf_count),
        "blk",
        scatter_dimension=0,
        tiled=True,
    )
    downward = jnp.transpose(spread.reshape(block_points, rhs_count, leaf_count), (1, 2, 0))
    window = 2 * HALO + 1
    total_leaves = leaf_count * lax.axis_size("leaf")
    leaf_global = first_leaf + jnp.arange(leaf_count, dtype=jnp.int32)
    window_start = jnp.clip(leaf_global - HALO, 0, total_leaves - window)
    window_rows = window_start - first_leaf + HALO
    near_offsets = near_list - window_start[:, None]
    near_pick = one_hot_rows(near_offsets, window)

    def near_leaf(leaf_pos):
        start_row = lax.dynamic_index_in_dim(window_rows, leaf_pos, 0, keepdims=False)
        window_data = lax.dynamic_slice_in_dim(extended, start_row, window, 1)
        pick_here = lax.dynamic_index_in_dim(near_pick, leaf_pos, 0, keepdims=False)
        picked = jnp.einsum(
            "crm,jr->cjm", window_data, pick_here, preferred_element_type=jnp.float32
        ).astype(jnp.bfloat16)
        picked = picked.reshape(extended.shape[0], NEAR * extended.shape[2])
        target = lax.dynamic_index_in_dim(points, leaf_pos, 1, keepdims=False)
        kernel = kernel_block(picked[:coord_count], target)
        return jnp.dot(picked[coord_count:], kernel, preferred_element_type=jnp.float32)

    near_field = jnp.transpose(
        lax.map(near_leaf, jnp.arange(leaf_count, dtype=jnp.int32)), (1, 0, 2)
    )
    return near_field + downward


def solution(mesh):
    placed = (
        P(None, "leaf", "blk"),
        P(None, "leaf", "blk"),
        P("leaf", None, None),
        P("leaf", None, None),
        P("leaf", None),
        P("leaf", None),
        P("leaf", None),
        P("leaf", None),
        P("leaf"),
    )
    return jax.shard_map(
        on_device, mesh=mesh, in_specs=placed, out_specs=P(None, "leaf", "blk"), check_vma=False
    )
```

profile of v0, /device:TPU:129, one launch (start us, length us, event | category | flops | bytes accessed | tf_op | source)
XLA Modules:
  0.0 495.5 jit_solution(17915731279965492917)
XLA Ops:
  12.7 29.7 %all-gather.3.cloned.1.call-done = bf16[80,16,512]{2,0,1:T(8,128)(2,1)} async-done(((bf16[80,16,128]{2,0,1:T(8,128)(2,1)}), bf16[80,16,512]{2,0,1:T(8,128)(2,1)}) %all-gather.3.cloned.1.call-update) | async-done | bytes 1310736 | tf_op jit(solution)/shard_map/all_gather | solution.py:71
  42.4 3.6 fusion.56
  46.0 2.5 fusion.55
  49.4 4.2 collective-permute-start.5
  53.7 3.7 collective-permute-start.4
  59.3 2.1 collective-permute-start.2
  65.0 2.7 collective-permute-start
  68.6 2.2 collective-permute-start.1
  70.8 4.6 collective-permute-done.4
  75.4 11.2 %collective-permute-done.2 = bf16[80,16,256]{2,0,1:T(8,128)(2,1)} collective-permute-done((bf16[80,16,256]{2,0,1:T(8,128)(2,1)}, bf16[80,16,256]{2,0,1:T(8,128)(2,1)}, u32[]{:S(2)}, u32[]{:S(2)}) %collective-permute-start.2) | collective-permute-done | bytes 655392 | tf_op jit(solution)/shard_map/ppermute | solution.py:30
  88.5 10.0 %convert_bitcast_fusion = bf16[80,16,32,256]{3,2,1,0:T(8,128)(2,1)} fusion(bf16[80,64,256,1]{2,0,1,3:T(8,128)(2,1)S(1)} %maximum_bitcast_fusion, s32[16,32]{1,0:T(8,128)S(1)} %add_clamp_fusion), kind=kOutput, calls=%fused_computation.49 | convolution fusion | flops 1352695808 | bytes 23595008 | tf_op jit(solution)/shard_map/crs,ljr->cljs/dot_general | solution.py:117
  98.5 162.6 %while.22 = (s32[]{:T(128)}, f32[16,16,64]{2,1,0:T(8,128)}, s32[16]{0:T(128)S(1)}, bf16[80,16,32,256]{3,2,1,0:T(8,128)(2,1)}, s32[16]{0:T(128)S(1)}, /*index=5*/...) while((s32[]{:T(128)}, f32[16,16,64]{2,1,0:T(8,128)}, s32[16]{0:T(128)S(1)}, ...), condition=%wide.region_7.8_spmd.clone, body=%wide.region_4.7_spmd.clone.sunk | while | flops 87568424 | bytes 6817039 | solution.py:131
  106.5 2.2 fusion.121
  116.7 2.2 fusion.121
  126.8 2.2 fusion.121
  137.0 2.2 fusion.121
  147.1 2.2 fusion.121
  157.3 2.2 fusion.121
  167.5 2.2 fusion.121
  177.6 2.2 fusion.121
  187.8 2.2 fusion.121
  198.0 2.2 fusion.121
  208.1 2.2 fusion.121
  218.3 2.2 fusion.121
  228.4 2.2 fusion.121
  238.6 2.2 fusion.121
  248.8 2.2 fusion.121
  258.9 2.2 fusion.121
  261.1 3.5 pad_maximum_fusion
  264.6 2.1 multiply_reduce_fusion.4
  266.8 7.5 %fusion.62 = bf16[16,256,1]{1,0,2:T(8,128)(2,1)S(1)} fusion(bf16[64,256]{1,0:T(8,128)(2,1)S(1)} %copy-done.6, f32[256]{0:T(256)S(1)} %broadcast_multiply_fusion.4, f32[16384]{0:T(1024)S(1)} %broadcast_multiply_fusion.3, pred[16384]{0:T(1024)(128)(4,1)S(1)} %fusion.76, bf16[80,16384]{1,0:T(8,128)(2,1)} %all-gather.5.cloned.1.call-done), kind=kOutput, calls=%fused_computation.73 | convolution fusion | flops 687869952 | bytes 2745344 | tf_op jit(solution)/shard_map/dot_general | solution.py:100
  277.3 210.1 %while.21 = (s32[]{:T(128)}, f32[16,16,128]{2,0,1:T(8,128)}, s32[16]{0:T(128)S(1)}, bf16[16,10,17]{2,1,0:T(8,128)(2,1)S(1)}, s32[16]{0:T(128)S(1)}, /*index=5*/b...) while((s32[]{:T(128)}, f32[16,16,128]{2,0,1:T(8,128)}, ...), condition=%wide.region_3.4_spmd, body=%wide.region_0.0_spmd.sunk | while | flops 122167304 | bytes 9935077 | solution.py:167
  287.0 2.0 fusion.117
  300.1 1.9 fusion.117
  313.2 1.9 fusion.117
  326.4 1.9 fusion.117
  339.5 2.0 fusion.117
  352.6 1.9 fusion.117
  365.8 1.9 fusion.117
  378.9 1.9 fusion.117
  392.0 2.0 fusion.117
  405.1 1.9 fusion.117
  418.3 1.9 fusion.117
  431.4 1.9 fusion.117
  444.5 2.0 fusion.117
  457.6 1.9 fusion.117
  470.8 1.9 fusion.117
  483.9 1.9 fusion.117
  (491 shorter events, 232.7 us)
Async XLA Ops:
  6.5 54.9 %copy-start = (bf16[16,256,256]{2,1,0:T(8,128)(2,1)S(1)}, bf16[16,256,256]{2,1,0:T(8,128)(2,1)}, u32[]{:S(2)}) copy-start(bf16[16,256,256]{2,1,0:T(8,128)(2,1)} %param.16) | copy-start | bytes 6291460
  6.5 35.9 %all-gather.3.cloned.1.call-start = ((), (), s32[]{:S(2)}) async-start(), calls=%async_computation.1 | async-start | bytes 1638400 | tf_op jit(solution)/shard_map/all_gather | solution.py:71
  11.0 35.0 %copy-start.7 = (s32[16,256]{1,0:T(8,128)S(1)}, s32[16,256]{1,0:T(8,128)}, u32[]{:S(2)}) copy-start(s32[16,256]{1,0:T(8,128)} %param.17) | copy-start | bytes 49156
  11.0 253.6 %all-gather.5.cloned.1.call-start = ((), (), s32[]{:S(2)}) async-start(), calls=%async_computation.2 | async-start | bytes 2662400 | tf_op jit(solution)/shard_map/all_gather | solution.py:94
  42.4 3.6 copy-start.1
  48.5 14.7 %copy-start.2 = (bf16[16,256,64]{1,2,0:T(8,128)(2,1)}, bf16[16,256,64]{1,2,0:T(8,128)(2,1)S(1)}, u32[]{:S(2)}) copy-start(bf16[16,256,64]{1,2,0:T(8,128)(2,1)S(1)} %fusion.55) | copy-start | bytes 1572868
  48.5 13.7 %copy-start.8 = (s32[1,256]{1,0:T(1,128)S(1)}, s32[1,256]{1,0:T(1,128)}, u32[]{:S(2)}) copy-start(s32[1,256]{1,0:T(1,128)} %param.18) | copy-start | bytes 3076
  49.4 19.1 %collective-permute-start.5 = (bf16[80,16,256]{2,0,1:T(8,128)(2,1)}, bf16[80,16,256]{2,0,1:T(8,128)(2,1)}, u32[]{:S(2)}, u32[]{:S(2)}) collective-permute-start(bf16[80,16,256]{2,0,1:T(8,128)(2,1)} %pad_maximum_fusion.1), channel_id=1, source_target_pairs={{8,0},{12,4},{16,8},{20,12},{24,16},{28,20},{32,24},{36,28},{40,32... | collective-permute-start | bytes 1966088 | tf_op jit(solution)/shard_map/ppermute | solution.py:30
  53.7 21.7 %collective-permute-start.4 = (bf16[80,16,256]{2,0,1:T(8,128)(2,1)}, bf16[80,16,256]{2,0,1:T(8,128)(2,1)}, u32[]{:S(2)}, u32[]{:S(2)}) collective-permute-start(bf16[80,16,256]{2,0,1:T(8,128)(2,1)} %pad_maximum_fusion.1), channel_id=1, source_target_pairs={{4,0},{8,4},{12,8},{16,12},{20,16},{24,20},{28,24},{32,28},{36,32}... | collective-permute-start | bytes 1966088 | tf_op jit(solution)/shard_map/ppermute | solution.py:30
  57.4 18.0 %collective-permute-start.3 = (bf16[80,16,256]{2,0,1:T(8,128)(2,1)}, bf16[80,16,256]{2,0,1:T(8,128)(2,1)}, u32[]{:S(2)}, u32[]{:S(2)}) collective-permute-start(bf16[80,16,256]{2,0,1:T(8,128)(2,1)} %pad_maximum_fusion.1), channel_id=1, source_target_pairs={{0,4},{4,8},{8,12},{12,16},{16,20},{20,24},{24,28},{28,32},{32,36}... | collective-permute-start | bytes 1966088 | tf_op jit(solution)/shard_map/ppermute | solution.py:30
  59.3 27.3 %collective-permute-start.2 = (bf16[80,16,256]{2,0,1:T(8,128)(2,1)}, bf16[80,16,256]{2,0,1:T(8,128)(2,1)}, u32[]{:S(2)}, u32[]{:S(2)}) collective-permute-start(bf16[80,16,256]{2,0,1:T(8,128)(2,1)} %pad_maximum_fusion.1), channel_id=1, source_target_pairs={{0,8},{4,12},{8,16},{12,20},{16,24},{20,28},{24,32},{28,36},{32,40... | collective-permute-start | bytes 1966088 | tf_op jit(solution)/shard_map/ppermute | solution.py:30
  63.1 25.3 %copy-start.5 = (bf16[64,256]{1,0:T(8,128)(2,1)}, bf16[64,256]{1,0:T(8,128)(2,1)S(1)}, u32[]{:S(2)}) copy-start(bf16[64,256]{1,0:T(8,128)(2,1)S(1)} %get-tuple-element.153) | copy-start | bytes 98308
  63.8 423.6 %reduce-scatter.2.cloned.1.call-start = ((), (), s32[]{:S(2)}) async-start(), calls=%async_computation.3 | async-start | bytes 655360 | tf_op jit(solution)/shard_map/reduce_scatter | solution.py:139
  63.8 3.9 copy-start.3
  65.0 196.1 %collective-permute-start = (bf16[80,8,512]{2,0,1:T(8,128)(2,1)}, bf16[80,8,512]{2,0,1:T(8,128)(2,1)}, u32[]{:S(2)}, u32[]{:S(2)}) collective-permute-start(bf16[80,8,512]{2,0,1:T(8,128)(2,1)} %get-tuple-element.150), channel_id=1, source_target_pairs={{0,4},{4,8},{8,12},{12,16},{16,20},{20,24},{24,28},{28,32},{32,36}... | collective-permute-start | bytes 1966088 | tf_op jit(solution)/shard_map/ppermute | solution.py:19
  68.6 192.5 %collective-permute-start.1 = (bf16[80,8,512]{2,0,1:T(8,128)(2,1)}, bf16[80,8,512]{2,0,1:T(8,128)(2,1)}, u32[]{:S(2)}, u32[]{:S(2)}) collective-permute-start(bf16[80,8,512]{2,0,1:T(8,128)(2,1)} %get-tuple-element.151), channel_id=1, source_target_pairs={{4,0},{8,4},{12,8},{16,12},{20,16},{24,20},{28,24},{32,28},{36,32}... | collective-permute-start | bytes 1966088 | tf_op jit(solution)/shard_map/ppermute | solution.py:22
  88.5 10.0 %copy-start.9 = (s32[16]{0:T(128)S(1)}, s32[16]{0:T(128)}, u32[]{:S(2)}) copy-start(s32[16]{0:T(128)} %param.21) | copy-start | bytes 196
  261.1 5.6 %copy-start.6 = (bf16[64,256]{1,0:T(8,128)(2,1)S(1)}, bf16[64,256]{1,0:T(8,128)(2,1)}, u32[]{:S(2)}) copy-start(bf16[64,256]{1,0:T(8,128)(2,1)} %copy-done.5) | copy-start | bytes 98308
  266.8 7.5 %copy-start.4 = (f32[16,16,64]{2,1,0:T(8,128)S(1)}, f32[16,16,64]{2,1,0:T(8,128)}, u32[]{:S(2)}) copy-start(f32[16,16,64]{2,1,0:T(8,128)} %get-tuple-element.80) | copy-start | bytes 196612
Sparse Core Ops, SparseCore 0:
  11.1 31.2 all-gather.2
  63.9 74.3 all-gather.4
  277.4 20.3 reduce-scatter.1
where the time goes:
time: 503 us; the launch traced here: 496 us
  local copies, waits for them, and re-layouts  132 us (26%)
  matrix products  118 us (23%)
  loops' own time  93.6 us (19%)
  other arithmetic  76.8 us (15%)
  waiting for transfers between devices  45.5 us (9%)
  starting transfers between devices  17 us (3%)
  between operations  13.4 us (3%)
    another operation x1, loops' own time, on_device(): lax.map(near_leaf, jnp.arange(leaf_count, dtype=jnp.int32))  63 us
    dot_general x16, matrix products, far_leaf(): jnp.dot(picked[coord_count:], kernel, preferred_element_type=jnp.float32)  35 us
    dot_general x16, matrix products, near_leaf(): jnp.dot(picked[coord_count:], kernel, preferred_element_type=jnp.float32)  31.2 us
    another operation x1, loops' own time, on_device(): far_field = lax.map(far_leaf, jnp.arange(leaf_count, dtype=jnp.int32))  30.6 us
    reduce_sum x33, other arithmetic, kernel_block(): source_norm = jnp.sum(jnp.square(sources.astype(jnp.float32)), axis=0)  30.5 us
    all_gather x1, waiting for transfers between devices, on_device(): gathered = lax.all_gather(stacked, 'blk', axis=2, tiled=True)  29.7 us
    dot_general x16, matrix products, near_leaf(): jnp.einsum('crm,jr->cjm', window_data, pick_here, preferred_element_type=...  24.5 us
    dynamic_update_slice x16, local copies, waits for them, and re-layouts, on_device(): lax.map(near_leaf, jnp.arange(leaf_count, dtype=jnp.int32))  24.1 us
  transfers between devices with their start and end apart: 9, of which 3 were waited for; matrix products, arithmetic and copies ran while one was open for 61% of the time, Pallas kernels for 0%

commit v1 on v0

v1 whole, which is shorter than its diff:
```python
import jax
import jax.numpy as jnp
from jax import lax
from jax.experimental import pallas as pl
from jax.experimental.pallas import tpu as pltpu
from jax.sharding import PartitionSpec as P

MESH = pl.DeviceIdType.MESH
F32 = jnp.float32
BF16 = jnp.bfloat16
NT = (((1,), (1,)), ((), ()))

DIM = 64
RHS = 16
RAW = DIM + RHS
ROWS = 96
LEAVES = 16
PTS = 128
BLKS = 4
SKEL = 256
HALO = 8
NEAR = 10
FAR = 32
OWNERS = 64
CHUNKS = 4
CHUNK = LEAVES // CHUNKS
STEPS = (-2, -1, 1, 2)
GROUP = 8
VMEM_LIMIT = 58 * 2**20


def aug_rows(points):
    p = points.astype(F32)
    n = -0.5 * jnp.sum(p * p, axis=0, keepdims=True)
    hi = n.astype(BF16).astype(F32)
    rest = n - hi
    mid = rest.astype(BF16).astype(F32)
    low = rest - mid
    row = lax.broadcasted_iota(jnp.int32, (16, n.shape[1]), 0)
    out = jnp.where(row == 0, hi, jnp.where(row == 1, mid, jnp.where(row == 2, low, 0.0)))
    out = jnp.where((row >= 4) & (row < 7), 1.0, out)
    return out.astype(BF16)


def to_rows(points, aug):
    a = aug.astype(F32)[:8]
    swapped = jnp.concatenate([a[4:], a[:4]], axis=0)
    z16 = jnp.zeros((16, 128), F32)
    z40 = jnp.zeros((40, 128), F32)
    full = jnp.concatenate([points.astype(F32), z16, swapped, z40], axis=0)
    return full.T.astype(BF16)


def leaf_id(z, x, c):
    return (z * 4 + x) * 2 + c


def exchange_kernel(
    own, nl, si, ri, li_hbm, rt_hbm,
    near_o, skel_o, fs_o, wl_o, wr_o, root_o, rts_o,
    gath, halo, srow, swgt, li, rt, fout, fin, rbuf,
    li_sem, rt_sem, y_send, y_recv, f_send, f_recv, h_send, h_recv,
    far_send, far_recv, z_send, z_recv, x_send, x_recv, c_send, c_recv,
):
    o = lax.axis_index("leaf")
    b = lax.axis_index("blk")
    core = lax.rem(o, 2)
    cx = lax.rem(o // 2, 4)
    cz = o // 8
    up = lax.rem(b + 1, BLKS)
    down = lax.rem(b + BLKS - 1, BLKS)
    half = lax.rem(b, 2)
    parity = b // 2
    sender = core == parity

    li_copy = pltpu.make_async_copy(li_hbm, li, li_sem)
    rt_copy = pltpu.make_async_copy(rt_hbm, rt, rt_sem)
    li_copy.start()
    rt_copy.start()

    barrier = pltpu.get_barrier_semaphore()

    def greet(leaf, blk):
        pl.semaphore_signal(barrier, inc=1, device_id=(leaf, blk), device_id_type=MESH)

    greet(o, up)
    greet(o, down)
    for d in range(1, 8):
        greet(leaf_id(lax.rem(cz + d, 8), cx, core), b)
    for d in range(1, 4):
        greet(leaf_id(cz, lax.rem(cx + d, 4), core), b)
    greet(leaf_id(cz, cx, 1 - core), b)
    for step in STEPS:
        @pl.when((o + step >= 0) & (o + step < OWNERS))
        def _():
            greet(o + step, b)
    pl.semaphore_wait(barrier, 13 + jnp.minimum(o, 2) + jnp.minimum(OWNERS - 1 - o, 2))

    def remote(src, dst, ssem, rsem, leaf, blk):
        return pltpu.make_async_remote_copy(
            src_ref=src, dst_ref=dst, send_sem=ssem, recv_sem=rsem,
            device_id=(leaf, blk), device_id_type=MESH)

    has_low = o > 0
    has_high = o < OWNERS - 1
    h_up = remote(own.at[pl.ds(LEAVES - HALO, HALO)], halo.at[0], h_send.at[0], h_recv.at[0], o + 1, b)
    h_down = remote(own.at[pl.ds(0, HALO)], halo.at[1], h_send.at[1], h_recv.at[1], o - 1, b)

    @pl.when(has_high)
    def _():
        h_up.start()

    @pl.when(has_low)
    def _():
        h_down.start()

    def leaves(c):
        return pl.ds(c * CHUNK, CHUNK)

    direct = []
    for c in range(CHUNKS):
        pair = []
        for k, to in enumerate((up, down)):
            pair.append(remote(
                own.at[leaves(c)], gath.at[b, leaves(c), pl.ds(0, RAW)],
                y_send.at[c, k], y_recv.at[c, k], o, to))
        direct.append(pair)
        pair[0].start()
        pair[1].start()

    def forward(c, k):
        src = (down, up)[k]
        to = (up, down)[k]
        part = pl.ds(c * CHUNK + k * (CHUNK // 2), CHUNK // 2)
        ref = gath.at[src, part, pl.ds(0, RAW)]
        return remote(ref, ref, f_send.at[c, k], f_recv.at[c, k], o, to)

    @pl.loop(0, LEAVES)
    def _(l):
        raw = own[l]
        aug = aug_rows(raw[:DIM])
        gath[b, l, 0:RAW, :] = raw
        gath[b, l, RAW:ROWS, :] = aug
        srow[HALO + l] = to_rows(raw[:DIM], aug)
        swgt[HALO + l] = raw[DIM:]

    def take_halo(side, at):
        @pl.loop(0, HALO)
        def _(l):
            raw = halo[side, l]
            srow[at + l] = to_rows(raw[:DIM], aug_rows(raw[:DIM]))
            swgt[at + l] = raw[DIM:]

    def no_halo(at):
        @pl.loop(0, HALO)
        def _(l):
            srow[at + l] = jnp.zeros((128, 128), BF16)
            swgt[at + l] = jnp.zeros((RHS, 128), BF16)

    @pl.when(has_low)
    def _():
        h_up.wait_recv()
        take_halo(0, 0)

    @pl.when(jnp.logical_not(has_low))
    def _():
        no_halo(0)

    @pl.when(has_high)
    def _():
        h_down.wait_recv()
        take_halo(1, HALO + LEAVES)

    @pl.when(jnp.logical_not(has_high))
    def _():
        no_halo(HALO + LEAVES)

    near_base = HALO - o * LEAVES

    def near_leaf(l):
        ids = [jnp.clip(nl[l, j] + near_base, 0, 2 * HALO + LEAVES - 1) for j in range(NEAR)]
        s = jnp.concatenate([srow[i] for i in ids], axis=0)[:, :ROWS]
        w = jnp.concatenate([swgt[i] for i in ids], axis=1)
        t = jnp.concatenate([gath[k, l] for k in range(BLKS)], axis=1)
        x = jnp.dot(s, t, preferred_element_type=F32)
        p = jnp.exp(x).astype(BF16)
        near_o[l] = jnp.dot(w, p, preferred_element_type=F32)

    def near_range(lo, hi):
        @pl.loop(lo, hi)
        def _(l):
            near_leaf(l)

    def skeleton_leaf(l):
        t = jnp.concatenate([gath[k, l] for k in range(BLKS)], axis=1)
        idx = si[pl.ds(l, 1), :]
        m = lax.broadcasted_iota(jnp.int32, (BLKS * PTS, SKEL), 0)
        hot = jnp.where(m == idx, 1.0, 0.0).astype(BF16)
        nat = jnp.dot(t, hot, preferred_element_type=F32)
        wgt = lax.dot_general(t[DIM:RAW], li[l], NT, preferred_element_type=F32)
        skel_o[l] = jnp.concatenate([nat[:DIM], wgt, nat[RAW:]], axis=0).astype(BF16)

    lane = lax.broadcasted_iota(jnp.int32, (ROWS, 128), 1)

    def quarter(l):
        v = skel_o[l].astype(F32)
        return jnp.where(parity == 0, v[:, :128], v[:, 128:])

    def far_pair(q):
        a = quarter(2 * q)
        c = quarter(2 * q + 1)
        a = jnp.where(half == 0, a, pltpu.roll(a, 64, axis=1))
        c = jnp.where(half == 1, c, pltpu.roll(c, 64, axis=1))
        fout[q] = jnp.where(lane < 64, a, c).astype(BF16)

    def far_copy(c, k):
        part = pl.ds(c * 2, 2)
        return remote(fout.at[part], fin.at[3 - k, part], far_send.at[c, k], far_recv.at[c, 3 - k],
                      o + STEPS[k], b)

    def far_wait(c, k):
        part = pl.ds(c * 2, 2)
        return remote(fout.at[part], fin.at[k, part], far_send.at[c, k], far_recv.at[c, k],
                      o + STEPS[k], b)

    li_copy.wait()
    opp = lax.rem(b + 2, BLKS)
    for c in range(CHUNKS):
        direct[c][0].wait_recv()
        forward(c, 0).start()
        direct[c][1].wait_recv()
        forward(c, 1).start()

        @pl.loop(c * CHUNK, (c + 1) * CHUNK)
        def _(l):
            gath[up, l, RAW:ROWS, :] = aug_rows(gath[up, l, 0:DIM, :])
            gath[down, l, RAW:ROWS, :] = aug_rows(gath[down, l, 0:DIM, :])

        forward(c, 0).wait_recv()
        forward(c, 1).wait_recv()

        @pl.loop(c * CHUNK, (c + 1) * CHUNK)
        def _(l):
            gath[opp, l, RAW:ROWS, :] = aug_rows(gath[opp, l, 0:DIM, :])
            skeleton_leaf(l)

        @pl.loop(c * 2, c * 2 + 2)
        def _(q):
            far_pair(q)

        for k, step in enumerate(STEPS):
            @pl.when((o + step >= 0) & (o + step < OWNERS))
            def _():
                far_copy(c, k).start()

        if c < CHUNKS - 1:
            near_range(c * CHUNK, c * CHUNK + 2)

    rt_copy.wait()
    ridx = ri[0:1, :]
    s_id = lax.broadcasted_iota(jnp.int32, (SKEL, SKEL), 0)

    def root_step(l, carry):
        pts, wgt = carry
        hot = jnp.where(s_id + l * SKEL == ridx, 1.0, 0.0).astype(BF16)
        pts = pts + jnp.dot(skel_o[l], hot, preferred_element_type=F32)
        rows = rt[l, pl.ds(pl.multiple_of(half * 128, 128), 128), :]
        wgt = wgt + lax.dot_general(skel_o[l, DIM:RAW, :], rows, NT, preferred_element_type=F32)
        return pts, wgt

    pts, wgt = lax.fori_loop(
        0, LEAVES, root_step, (jnp.zeros((ROWS, SKEL), F32), jnp.zeros((RHS, 128), F32)))
    mine = jnp.where(half == 0, pts[:, :128], pts[:, 128:])

    @pl.when(sender)
    def _():
        rbuf[cx, cz] = jnp.concatenate([mine[:DIM], wgt, mine[RAW:]], axis=0).astype(BF16)

    def root_z(d):
        to = leaf_id(lax.rem(cz + d, 8), cx, core)
        ref = rbuf.at[cx, cz]
        return remote(ref, ref, z_send.at[d - 1], z_recv.at[d - 1], to, b)

    def root_z_wait(d):
        src = lax.rem(cz + 8 - d, 8)
        ref = rbuf.at[cx, src]
        return remote(ref, ref, z_send.at[d - 1], z_recv.at[d - 1], leaf_id(src, cx, core), b)

    def root_x(d):
        to = leaf_id(cz, lax.rem(cx + d, 4), core)
        ref = rbuf.at[cx]
        return remote(ref, ref, x_send.at[d - 1], x_recv.at[d - 1], to, b)

    def root_x_wait(d):
        src = lax.rem(cx + 4 - d, 4)
        ref = rbuf.at[src]
        return remote(ref, ref, x_send.at[d - 1], x_recv.at[d - 1], leaf_id(cz, src, core), b)

    def root_c(d):
        ref = rbuf.at[lax.rem(cx + 4 - d, 4)]
        return remote(ref, ref, c_send.at[d], c_recv.at[d], leaf_id(cz, cx, 1 - core), b)

    @pl.when(sender)
    def _():
        for d in range(1, 8):
            root_z(d).start()

    for h in range(2):
        v = pts[:, h * 128:(h + 1) * 128]
        rts_o[h * 128:(h + 1) * 128, :] = to_rows(v[:DIM], v[RAW:])

    near_range(2, 4)
    near_range(6, 8)

    @pl.when(sender)
    def _():
        for d in range(1, 8):
            root_z_wait(d).wait_recv()
        for d in range(1, 4):
            root_x(d).start()
        root_c(0).start()

    near_range(10, 13)

    @pl.when(sender)
    def _():
        for d in range(1, 4):
            root_x_wait(d).wait_recv()
            root_c(d).start()

    near_range(13, 16)

    wlane = lax.broadcasted_iota(jnp.int32, (RHS, 128), 1)
    for k, step in enumerate(STEPS):
        exists = (o + step >= 0) & (o + step < OWNERS)

        @pl.when(exists)
        def _():
            for c in range(CHUNKS):
                far_wait(c, k).wait_recv()

            @pl.loop(0, 8)
            def _(q):
                v = fin[k, q]
                fs_o[k * 8 + q] = to_rows(v[:DIM], v[RAW:])
                w = v[DIM:RAW].astype(F32)
                left = jnp.where(wlane < 64, w, 0.0)
                right = jnp.where(wlane < 64, 0.0, w)
                even = k * 16 + 2 * q
                wl_o[even] = left.astype(BF16)
                wr_o[even] = pltpu.roll(left, 64, axis=1).astype(BF16)
                wl_o[even + 1] = pltpu.roll(right, 64, axis=1).astype(BF16)
                wr_o[even + 1] = right.astype(BF16)

        @pl.when(jnp.logical_not(exists))
        def _():
            @pl.loop(0, 8)
            def _(q):
                fs_o[k * 8 + q] = jnp.zeros((128, 128), BF16)
                for e in range(2):
                    wl_o[k * 16 + 2 * q + e] = jnp.zeros((RHS, 128), BF16)
                    wr_o[k * 16 + 2 * q + e] = jnp.zeros((RHS, 128), BF16)

    @pl.when(jnp.logical_not(sender))
    def _():
        for d in range(4):
            root_c(d).wait_recv()

    @pl.loop(0, 4)
    def _(x):
        @pl.loop(0, 8)
        def _(z):
            root_o[x * 8 + z] = rbuf[x, z]

    @pl.when(has_high)
    def _():
        h_up.wait_send()

    @pl.when(has_low)
    def _():
        h_down.wait_send()

    for c in range(CHUNKS):
        for k, step in enumerate(STEPS):
            @pl.when((o + step >= 0) & (o + step < OWNERS))
            def _():
                far_copy(c, k).wait_send()
        for k in range(2):
            direct[c][k].wait_send()
            forward(c, k).wait_send()

    @pl.when(sender)
    def _():
        for d in range(1, 8):
            root_z(d).wait_send()
        for d in range(1, 4):
            root_x(d).wait_send()
        for d in range(4):
            root_c(d).wait_send()


def field_kernel(place, table, count, near, skel, fs, wl, wr, root, rts, li_hbm, rt_hbm, part, li, rt, li_sem, rt_sem):
    li_copy = pltpu.make_async_copy(li_hbm, li, li_sem)
    rt_copy = pltpu.make_async_copy(rt_hbm, rt, rt_sem)
    rt_copy.start()
    li_copy.start()
    o = place[0]
    b = place[1]
    parity = b // 2

    targets = rts[:, :ROWS]

    def root_pair(i, acc):
        cols = []
        wgts = []
        for e in range(2):
            k = 2 * i + e
            x = k // 8
            z = k - x * 8
            p = (z * 4 + x) * 2 + parity
            v = root[k]
            cols.append(v)
            wgts.append(jnp.where(jnp.abs(p - o) > 2, v[DIM:RAW].astype(F32), 0.0).astype(BF16))
        xt = jnp.dot(targets, jnp.concatenate(cols, axis=1), preferred_element_type=F32)
        pt = jnp.exp(xt).astype(BF16)
        w = jnp.concatenate(wgts, axis=1)
        return acc + lax.dot_general(w, pt, NT, preferred_element_type=F32)

    rf = lax.fori_loop(0, 16, root_pair, jnp.zeros((RHS, SKEL), F32), unroll=4).astype(BF16)
    rt_copy.wait()
    li_copy.wait()

    @pl.loop(0, LEAVES)
    def _(l):
        n = count[l]
        t = skel[l]

        def group(g, acc):
            ids = [table[l, g * GROUP + j] for j in range(GROUP)]
            s = jnp.concatenate([fs[i] for i in ids], axis=0)[:, :ROWS]
            ws = []
            for j in range(0, GROUP, 2):
                live0 = g * GROUP + j < n
                live1 = g * GROUP + j + 1 < n
                a = jnp.where(live0, wl[ids[j]].astype(F32), 0.0)
                c = jnp.where(live1, wr[ids[j + 1]].astype(F32), 0.0)
                ws.append((a + c).astype(BF16))
            w = jnp.concatenate(ws, axis=1)
            x = jnp.dot(s, t, preferred_element_type=F32)
            p = jnp.exp(x).astype(BF16)
            return acc + jnp.dot(w, p, preferred_element_type=F32)

        acc = jnp.dot(rf, rt[l], preferred_element_type=F32)
        acc = lax.fori_loop(0, (n + GROUP - 1) // GROUP, group, acc)
        out = near[l] + jnp.dot(acc.astype(BF16), li[l], preferred_element_type=F32)
        out = out.astype(BF16)
        for d in range(BLKS):
            part[d, l] = out[:, d * 128:(d + 1) * 128]


def scatter_kernel(part, out, land, send, recv):
    o = lax.axis_index("leaf")
    b = lax.axis_index("blk")
    barrier = pltpu.get_barrier_semaphore()
    for d in range(1, BLKS):
        pl.semaphore_signal(barrier, inc=1, device_id=(o, lax.rem(b + d, BLKS)), device_id_type=MESH)
    pl.semaphore_wait(barrier, BLKS - 1)
    copies = []
    for d in (2, 1, 3):
        to = lax.rem(b + d, BLKS)
        copy = pltpu.make_async_remote_copy(
            src_ref=part.at[to], dst_ref=land.at[d - 1], send_sem=send.at[d - 1],
            recv_sem=recv.at[d - 1], device_id=(o, to), device_id_type=MESH)
        copy.start()
        copies.append(copy)
    for copy in copies:
        copy.wait_recv()
    for l in range(LEAVES):
        total = part[b, l].astype(F32)
        for d in range(BLKS - 1):
            total = total + land[d, l].astype(F32)
        out[:, l, :] = total
    for copy in copies:
        copy.wait_send()


def on_device(points, charges, leaf_interp, root_interp, skeleton_index, root_index, near_list, far_list, far_count):
    o = lax.axis_index("leaf").astype(jnp.int32)
    b = lax.axis_index("blk").astype(jnp.int32)
    own = jnp.transpose(jnp.concatenate([points, charges], axis=0), (1, 0, 2))
    vmem = pl.BlockSpec(memory_space=pltpu.VMEM)
    smem = pl.BlockSpec(memory_space=pltpu.SMEM)
    hbm = pl.BlockSpec(memory_space=pl.ANY)
    dma = pltpu.SemaphoreType.DMA

    near, skel, fs, wl, wr, root, rts = pl.pallas_call(
        exchange_kernel,
        out_shape=(
            jax.ShapeDtypeStruct((LEAVES, RHS, BLKS * PTS), F32),
            jax.ShapeDtypeStruct((LEAVES, ROWS, SKEL), BF16),
            jax.ShapeDtypeStruct((32, 128, 128), BF16),
            jax.ShapeDtypeStruct((64, RHS, 128), BF16),
            jax.ShapeDtypeStruct((64, RHS, 128), BF16),
            jax.ShapeDtypeStruct((32, ROWS, 128), BF16),
            jax.ShapeDtypeStruct((SKEL, 128), BF16),
        ),
        in_specs=[vmem, smem, vmem, vmem, hbm, hbm],
        out_specs=(vmem,) * 7,
        scratch_shapes=[
            pltpu.VMEM((BLKS, LEAVES, ROWS, PTS), BF16),
            pltpu.VMEM((2, HALO, RAW, PTS), BF16),
            pltpu.VMEM((2 * HALO + LEAVES, 128, 128), BF16),
            pltpu.VMEM((2 * HALO + LEAVES, RHS, 128), BF16),
            pltpu.VMEM((LEAVES, SKEL, BLKS * PTS), BF16),
            pltpu.VMEM((LEAVES, SKEL, SKEL), BF16),
            pltpu.VMEM((8, ROWS, 128), BF16),
            pltpu.VMEM((4, 8, ROWS, 128), BF16),
            pltpu.VMEM((4, 8, ROWS, 128), BF16),
            dma, dma,
            dma((CHUNKS, 2)), dma((CHUNKS, 2)), dma((CHUNKS, 2)), dma((CHUNKS, 2)),
            dma((2,)), dma((2,)),
            dma((CHUNKS, 4)), dma((CHUNKS, 4)),
            dma((7,)), dma((7,)), dma((3,)), dma((3,)), dma((4,)), dma((4,)),
        ],
        compiler_params=pltpu.CompilerParams(
            collective_id=0, has_side_effects=True, vmem_limit_bytes=VMEM_LIMIT),
    )(own, near_list, skeleton_index, root_index, leaf_interp, root_interp)

    source_owner = far_list // LEAVES
    offset = source_owner - o
    table = (offset + 2 - (offset > 0).astype(jnp.int32)) * LEAVES + far_list - source_owner * LEAVES
    live = jnp.arange(FAR, dtype=jnp.int32)[None, :] < far_count[:, None]
    table = jnp.clip(jnp.where(live, table, table[:, :1]), 0, 63)
    place = jnp.stack([o, b])

    part = pl.pallas_call(
        field_kernel,
        out_shape=jax.ShapeDtypeStruct((BLKS, LEAVES, RHS, PTS), BF16),
        in_specs=[smem, smem, smem, vmem, vmem, vmem, vmem, vmem, vmem, vmem, hbm, hbm],
        out_specs=vmem,
        scratch_shapes=[
            pltpu.VMEM((LEAVES, SKEL, BLKS * PTS), BF16),
            pltpu.VMEM((LEAVES, SKEL, SKEL), BF16),
            dma, dma,
        ],
        compiler_params=pltpu.CompilerParams(vmem_limit_bytes=VMEM_LIMIT),
    )(place, table, far_count, near, skel, fs.reshape(64, 64, 128), wl, wr, root, rts, leaf_interp, root_interp)

    return pl.pallas_call(
        scatter_kernel,
        out_shape=jax.ShapeDtypeStruct((RHS, LEAVES, PTS), F32),
        in_specs=[vmem],
        out_specs=vmem,
        scratch_shapes=[
            pltpu.VMEM((BLKS - 1, LEAVES, RHS, PTS), BF16),
            dma((BLKS - 1,)), dma((BLKS - 1,)),
        ],
        compiler_params=pltpu.CompilerParams(
            collective_id=1, has_side_effects=True, vmem_limit_bytes=VMEM_LIMIT),
    )(part)


def solution(mesh):
    placed = (
        P(None, "leaf", "blk"),
        P(None, "leaf", "blk"),
        P("leaf", None, None),
        P("leaf", None, None),
        P("leaf", None),
        P("leaf", None),
        P("leaf", None),
        P("leaf", None),
        P("leaf"),
    )
    return jax.shard_map(
        on_device, mesh=mesh, in_specs=placed, out_specs=P(None, "leaf", "blk"), check_vma=False
    )
```

time: 503 us -> 100 us (0.20)
  the two profiles are of different devices: /device:TPU:129 before, /device:TPU:68 now
where the time goes in v1:
time: 100 us; the launch traced here: 99.8 us
  Pallas kernels  94.1 us (94%)
  local copies, waits for them, and re-layouts  3.59 us (4%)
  other arithmetic  2.1 us (2%)
    pallas_call x1, Pallas kernels, on_device(): pl.pallas_call(exchange_kernel, out_shape=(jax.ShapeDtypeStruct((LEAVES,...  60.5 us
    pallas_call x1, Pallas kernels, on_device(): pl.pallas_call(field_kernel, out_shape=jax.ShapeDtypeStruct((BLKS, LEAVES...  25.2 us
    pallas_call x1, Pallas kernels, on_device(): pl.pallas_call(scatter_kernel, out_shape=jax.ShapeDtypeStruct((RHS, LEAVE...  8.36 us
    unnamed x7, local copies, waits for them, and re-layouts  3.48 us

profile of v1, /device:TPU:68, one launch (start us, length us, event | category | flops | bytes accessed | tf_op | source)
XLA Modules:
  0.0 99.8 jit_solution(17902124918896243727)
XLA Ops:
  0.0 0.0 copy-start
  0.0 0.0 copy-start.1
  0.0 1.0 %copy.12 = bf16[64,16,128]{2,0,1:T(8,128)(2,1)S(1)} copy(bf16[64,16,128]{2,1,0:T(8,128)(2,1)} %param.9) | data formatting | bytes 524288 | tf_op args[0]
  1.1 0.9 copy.13
  1.9 0.7 maximum_bitcast_fusion.own
  2.7 60.5 %shard_map.91 = (f32[16,16,512]{2,1,0:T(8,128)}, bf16[16,96,256]{2,1,0:T(8,128)(2,1)}, bf16[32,128,128]{2,1,0:T(8,128)(2,1)}, bf16[64,16,128]{2,1,0:T(8,128)(2,1...) custom-call(bf16[16,80,128]{2,1,0:T(8,128)(2,1)} %maximum_bitcast_fusion.own, ...), custom_call_target="tpu_custom_call" | custom-call | tf_op jit(solution)/shard_map/pallas_call | solution.py:496
  63.2 0.0 copy-done
  63.2 0.1 slice_reduce_fusion
  63.4 0.0 copy-done.1
  63.4 0.7 select_clamp_fusion.table
  64.0 0.7 pad_add_fusion.place
  64.7 25.2 %shard_map.92.part = bf16[4,16,16,128]{3,2,1,0:T(8,128)(2,1)} custom-call(s32[2]{0:T(128)} %pad_add_fusion.place, s32[16,32]{1,0:T(8,128)} %select_clamp_fusion.table, s32[16]{0:T(128)} %count.1, f32[16,16,512]{2,1,0:T(8,128)} %get-tuple-element.12.near, bf16[16,96,256]{2,1,0:T(8,128)(2,1)} %get-tuple-element.13.skel, bf16[64,64,128]{2,1,0:T(8,128)(2,1)} %bitcast.5, ...), custom_call_target="tpu_custom_call" | custom-call | tf_op jit(solution)/shard_map/pallas_call | solution.py:536
  89.9 8.4 %shard_map.93 = f32[16,16,128]{2,1,0:T(8,128)} custom-call(bf16[4,16,16,128]{3,2,1,0:T(8,128)(2,1)} %shard_map.92.part), custom_call_target="tpu_custom_call" | custom-call | tf_op jit(solution)/shard_map/pallas_call | solution.py:549
  98.3 1.6 %copy.15 = f32[16,16,128]{2,1,0:T(8,128)} copy(f32[16,16,128]{2,1,0:T(8,128)} %shard_map.93) | data formatting | bytes 262144
  (1 shorter events, 0.0 us)
Async XLA Ops:
  0.0 63.2 %copy-start = (s32[16,32]{1,0:T(8,128)S(1)}, s32[16,32]{1,0:T(8,128)}, u32[]{:S(2)}) copy-start(s32[16,32]{1,0:T(8,128)} %param.16) | copy-start | bytes 6148
  0.0 63.4 %copy-start.1 = (s32[16]{0:T(128)S(1)}, s32[16]{0:T(128)}, u32[]{:S(2)}) copy-start(s32[16]{0:T(128)} %count.1) | copy-start | bytes 196

commit v2 on v1

--- a/solution.py
+++ b/solution.py
@@ -24,8 +24,9 @@
 OWNERS = 64
 CHUNKS = 4
 CHUNK = LEAVES // CHUNKS
+AHEAD = 2
 STEPS = (-2, -1, 1, 2)
-GROUP = 8
+PAIRS = FAR // 2
 VMEM_LIMIT = 58 * 2**20
 
 
@@ -55,12 +56,13 @@
     return (z * 4 + x) * 2 + c
 
 
-def exchange_kernel(
-    own, nl, si, ri, li_hbm, rt_hbm,
-    near_o, skel_o, fs_o, wl_o, wr_o, root_o, rts_o,
+def potential_kernel(
+    own, nl, fl_s, fl_v, si, ri, li_hbm, rt_hbm,
+    out,
     gath, halo, srow, swgt, li, rt, fout, fin, rbuf,
+    near_o, skel_o, fs, wl, wr, rts, sall, wall, mask, farsum, part, land,
     li_sem, rt_sem, y_send, y_recv, f_send, f_recv, h_send, h_recv,
-    far_send, far_recv, z_send, z_recv, x_send, x_recv, c_send, c_recv,
+    far_send, far_recv, z_send, z_recv, x_send, x_recv, c_send, c_recv, s_send, s_recv,
 ):
     o = lax.axis_index("leaf")
     b = lax.axis_index("blk")
@@ -90,11 +92,12 @@
     for d in range(1, 4):
         greet(leaf_id(cz, lax.rem(cx + d, 4), core), b)
     greet(leaf_id(cz, cx, 1 - core), b)
+    greet(o, lax.rem(b + 2, BLKS))
     for step in STEPS:
         @pl.when((o + step >= 0) & (o + step < OWNERS))
         def _():
             greet(o + step, b)
-    pl.semaphore_wait(barrier, 13 + jnp.minimum(o, 2) + jnp.minimum(OWNERS - 1 - o, 2))
+    pl.semaphore_wait(barrier, 14 + jnp.minimum(o, 2) + jnp.minimum(OWNERS - 1 - o, 2))
 
     def remote(src, dst, ssem, rsem, leaf, blk):
         return pltpu.make_async_remote_copy(
@@ -125,8 +128,9 @@
                 own.at[leaves(c)], gath.at[b, leaves(c), pl.ds(0, RAW)],
                 y_send.at[c, k], y_recv.at[c, k], o, to))
         direct.append(pair)
-        pair[0].start()
-        pair[1].start()
+        if c < AHEAD:
+            pair[0].start()
+            pair[1].start()
 
     def forward(c, k):
         src = (down, up)[k]
@@ -225,36 +229,42 @@
 
     li_copy.wait()
     opp = lax.rem(b + 2, BLKS)
+
+    def chunk_work(c):
+        @pl.loop(c * CHUNK, (c + 1) * CHUNK)
+        def _(l):
+            gath[up, l, RAW:ROWS, :] = aug_rows(gath[up, l, 0:DIM, :])
+            gath[down, l, RAW:ROWS, :] = aug_rows(gath[down, l, 0:DIM, :])
+
+        forward(c, 0).wait_recv()
+        forward(c, 1).wait_recv()
+
+        @pl.loop(c * CHUNK, (c + 1) * CHUNK, unroll=2)
+        def _(l):
+            gath[opp, l, RAW:ROWS, :] = aug_rows(gath[opp, l, 0:DIM, :])
+            skeleton_leaf(l)
+
+        @pl.loop(c * 2, c * 2 + 2)
+        def _(q):
+            far_pair(q)
+
+        for k, step in enumerate(STEPS):
+            @pl.when((o + step >= 0) & (o + step < OWNERS))
+            def _():
+                far_copy(c, k).start()
+
     for c in range(CHUNKS):
         direct[c][0].wait_recv()
         forward(c, 0).start()
         direct[c][1].wait_recv()
         forward(c, 1).start()
-
-        @pl.loop(c * CHUNK, (c + 1) * CHUNK)
-        def _(l):
-            gath[up, l, RAW:ROWS, :] = aug_rows(gath[up, l, 0:DIM, :])
-            gath[down, l, RAW:ROWS, :] = aug_rows(gath[down, l, 0:DIM, :])
-
-        forward(c, 0).wait_recv()
-        forward(c, 1).wait_recv()
-
-        @pl.loop(c * CHUNK, (c + 1) * CHUNK)
-        def _(l):
-            gath[opp, l, RAW:ROWS, :] = aug_rows(gath[opp, l, 0:DIM, :])
-            skeleton_leaf(l)
-
-        @pl.loop(c * 2, c * 2 + 2)
-        def _(q):
-            far_pair(q)
-
-        for k, step in enumerate(STEPS):
-            @pl.when((o + step >= 0) & (o + step < OWNERS))
-            def _():
-                far_copy(c, k).start()
-
-        if c < CHUNKS - 1:
-            near_range(c * CHUNK, c * CHUNK + 2)
+        if c + AHEAD < CHUNKS:
+            direct[c + AHEAD][0].start()
+            direct[c + AHEAD][1].start()
+        if c > 0:
+            chunk_work(c - 1)
+            near_range((c - 1) * CHUNK, (c - 1) * CHUNK + 2)
+    chunk_work(CHUNKS - 1)
 
     rt_copy.wait()
     ridx = ri[0:1, :]
@@ -307,10 +317,11 @@
 
     for h in range(2):
         v = pts[:, h * 128:(h + 1) * 128]
-        rts_o[h * 128:(h + 1) * 128, :] = to_rows(v[:DIM], v[RAW:])
+        rts[h * 128:(h + 1) * 128, :] = to_rows(v[:DIM], v[RAW:])
 
     near_range(2, 4)
     near_range(6, 8)
+    near_range(10, 12)
 
     @pl.when(sender)
     def _():
@@ -320,15 +331,7 @@
             root_x(d).start()
         root_c(0).start()
 
-    near_range(10, 13)
-
-    @pl.when(sender)
-    def _():
-        for d in range(1, 4):
-            root_x_wait(d).wait_recv()
-            root_c(d).start()
-
-    near_range(13, 16)
+    near_range(12, 16)
 
     wlane = lax.broadcasted_iota(jnp.int32, (RHS, 128), 1)
     for k, step in enumerate(STEPS):
@@ -342,35 +345,115 @@
             @pl.loop(0, 8)
             def _(q):
                 v = fin[k, q]
-                fs_o[k * 8 + q] = to_rows(v[:DIM], v[RAW:])
+                even = k * 16 + 2 * q
+                rows = to_rows(v[:DIM], v[RAW:])
+                fs[even] = rows[:64]
+                fs[even + 1] = rows[64:]
                 w = v[DIM:RAW].astype(F32)
                 left = jnp.where(wlane < 64, w, 0.0)
                 right = jnp.where(wlane < 64, 0.0, w)
-                even = k * 16 + 2 * q
-                wl_o[even] = left.astype(BF16)
-                wr_o[even] = pltpu.roll(left, 64, axis=1).astype(BF16)
-                wl_o[even + 1] = pltpu.roll(right, 64, axis=1).astype(BF16)
-                wr_o[even + 1] = right.astype(BF16)
+                wl[even] = left
+                wr[even] = pltpu.roll(left, 64, axis=1)
+                wl[even + 1] = pltpu.roll(right, 64, axis=1)
+                wr[even + 1] = right
 
         @pl.when(jnp.logical_not(exists))
         def _():
-            @pl.loop(0, 8)
-            def _(q):
-                fs_o[k * 8 + q] = jnp.zeros((128, 128), BF16)
-                for e in range(2):
-                    wl_o[k * 16 + 2 * q + e] = jnp.zeros((RHS, 128), BF16)
-                    wr_o[k * 16 + 2 * q + e] = jnp.zeros((RHS, 128), BF16)
+            @pl.loop(k * 16, k * 16 + 16)
+            def _(e):
+                fs[e] = jnp.zeros((64, 128), BF16)
+                wl[e] = jnp.zeros((RHS, 128), F32)
+                wr[e] = jnp.zeros((RHS, 128), F32)
+
+    lists = fl_v[...]
+
+    def named(u):
+        f = fl_s[0, u]
+        owner = f // LEAVES
+        step = owner - o
+        at = (step + 2 - jnp.where(step > 0, 1, 0)) * LEAVES + f - owner * LEAVES
+        hit = jnp.max(jnp.where(lists == f, 1.0, 0.0), axis=1, keepdims=True)
+        return jnp.clip(at, 0, 63), hit * jnp.where(step == 0, 0.0, 1.0)
+
+    for v in range(PAIRS):
+        at0, hit0 = named(2 * v)
+        at1, hit1 = named(2 * v + 1)
+        sall[v * 128:v * 128 + 64, :] = fs[at0]
+        sall[v * 128 + 64:v * 128 + 128, :] = fs[at1]
+        wall[:, v * 128:(v + 1) * 128] = wl[at0] + wr[at1]
+        mask[:, v * 128:(v + 1) * 128] = jnp.where(wlane < 64, hit0, hit1)
+
+    def far_range(lo, hi):
+        @pl.loop(lo, hi, step=2)
+        def _(l):
+            t = jnp.concatenate([skel_o[l], skel_o[l + 1]], axis=1)
+            w0 = (wall[...] * mask[pl.ds(l, 1), :]).astype(BF16)
+            w1 = (wall[...] * mask[pl.ds(l + 1, 1), :]).astype(BF16)
+            x = jnp.dot(sall[:, :ROWS], t, preferred_element_type=F32)
+            p = jnp.exp(x).astype(BF16)
+            farsum[l] = jnp.dot(w0, p[:, :SKEL], preferred_element_type=F32)
+            farsum[l + 1] = jnp.dot(w1, p[:, SKEL:], preferred_element_type=F32)
+
+    far_range(0, 6)
+
+    @pl.when(sender)
+    def _():
+        for d in range(1, 4):
+            root_x_wait(d).wait_recv()
+            root_c(d).start()
+
+    far_range(6, 16)
 
     @pl.when(jnp.logical_not(sender))
     def _():
         for d in range(4):
             root_c(d).wait_recv()
 
-    @pl.loop(0, 4)
-    def _(x):
-        @pl.loop(0, 8)
-        def _(z):
-            root_o[x * 8 + z] = rbuf[x, z]
+    targets = rts[:, :ROWS]
+
+    def root_group(i, acc):
+        cols = []
+        wgts = []
+        for e in range(4):
+            x = i // 2
+            z = (i - 2 * x) * 4 + e
+            p = leaf_id(z, x, parity)
+            v = rbuf[x, z]
+            cols.append(v)
+            wgts.append(jnp.where(jnp.abs(p - o) > 2, v[DIM:RAW].astype(F32), 0.0).astype(BF16))
+        xt = jnp.dot(targets, jnp.concatenate(cols, axis=1), preferred_element_type=F32)
+        pt = jnp.exp(xt).astype(BF16)
+        w = jnp.concatenate(wgts, axis=1)
+        return acc + lax.dot_general(w, pt, NT, preferred_element_type=F32)
+
+    rf = lax.fori_loop(0, 8, root_group, jnp.zeros((RHS, SKEL), F32), unroll=2).astype(BF16)
+
+    def scatter_copy(c, d):
+        to = lax.rem(b + d, BLKS)
+        return remote(part.at[to, leaves(c)], land.at[d - 1, leaves(c)],
+                      s_send.at[c, d - 1], s_recv.at[c, d - 1], o, to)
+
+    for c in range(CHUNKS):
+        group = range(c * CHUNK, (c + 1) * CHUNK)
+        fields = [
+            (farsum[l] + jnp.dot(rf, rt[l], preferred_element_type=F32)).astype(BF16) for l in group
+        ]
+        for l, field in zip(group, fields):
+            total = near_o[l] + jnp.dot(field, li[l], preferred_element_type=F32)
+            total = total.astype(BF16)
+            for d in range(BLKS):
+                part[d, l] = total[:, d * 128:(d + 1) * 128]
+        for d in (2, 1, 3):
+            scatter_copy(c, d).start()
+
+    for c in range(CHUNKS):
+        for d in (1, 2, 3):
+            scatter_copy(c, d).wait_recv()
+        for l in range(c * CHUNK, (c + 1) * CHUNK):
+            total = part[b, l].astype(F32)
+            for d in range(BLKS - 1):
+                total = total + land[d, l].astype(F32)
+            out[l] = total
 
     @pl.when(has_high)
     def _():
@@ -385,6 +468,8 @@
             @pl.when((o + step >= 0) & (o + step < OWNERS))
             def _():
                 far_copy(c, k).wait_send()
+        for d in (1, 2, 3):
+            scatter_copy(c, d).wait_send()
         for k in range(2):
             direct[c][k].wait_send()
             forward(c, k).wait_send()
@@ -399,113 +484,18 @@
             root_c(d).wait_send()
 
 
-def field_kernel(place, table, count, near, skel, fs, wl, wr, root, rts, li_hbm, rt_hbm, part, li, rt, li_sem, rt_sem):
-    li_copy = pltpu.make_async_copy(li_hbm, li, li_sem)
-    rt_copy = pltpu.make_async_copy(rt_hbm, rt, rt_sem)
-    rt_copy.start()
-    li_copy.start()
-    o = place[0]
-    b = place[1]
-    parity = b // 2
-
-    targets = rts[:, :ROWS]
-
-    def root_pair(i, acc):
-        cols = []
-        wgts = []
-        for e in range(2):
-            k = 2 * i + e
-            x = k // 8
-            z = k - x * 8
-            p = (z * 4 + x) * 2 + parity
-            v = root[k]
-            cols.append(v)
-            wgts.append(jnp.where(jnp.abs(p - o) > 2, v[DIM:RAW].astype(F32), 0.0).astype(BF16))
-        xt = jnp.dot(targets, jnp.concatenate(cols, axis=1), preferred_element_type=F32)
-        pt = jnp.exp(xt).astype(BF16)
-        w = jnp.concatenate(wgts, axis=1)
-        return acc + lax.dot_general(w, pt, NT, preferred_element_type=F32)
-
-    rf = lax.fori_loop(0, 16, root_pair, jnp.zeros((RHS, SKEL), F32), unroll=4).astype(BF16)
-    rt_copy.wait()
-    li_copy.wait()
-
-    @pl.loop(0, LEAVES)
-    def _(l):
-        n = count[l]
-        t = skel[l]
-
-        def group(g, acc):
-            ids = [table[l, g * GROUP + j] for j in range(GROUP)]
-            s = jnp.concatenate([fs[i] for i in ids], axis=0)[:, :ROWS]
-            ws = []
-            for j in range(0, GROUP, 2):
-                live0 = g * GROUP + j < n
-                live1 = g * GROUP + j + 1 < n
-                a = jnp.where(live0, wl[ids[j]].astype(F32), 0.0)
-                c = jnp.where(live1, wr[ids[j + 1]].astype(F32), 0.0)
-                ws.append((a + c).astype(BF16))
-            w = jnp.concatenate(ws, axis=1)
-            x = jnp.dot(s, t, preferred_element_type=F32)
-            p = jnp.exp(x).astype(BF16)
-            return acc + jnp.dot(w, p, preferred_element_type=F32)
-
-        acc = jnp.dot(rf, rt[l], preferred_element_type=F32)
-        acc = lax.fori_loop(0, (n + GROUP - 1) // GROUP, group, acc)
-        out = near[l] + jnp.dot(acc.astype(BF16), li[l], preferred_element_type=F32)
-        out = out.astype(BF16)
-        for d in range(BLKS):
-            part[d, l] = out[:, d * 128:(d + 1) * 128]
-
-
-def scatter_kernel(part, out, land, send, recv):
-    o = lax.axis_index("leaf")
-    b = lax.axis_index("blk")
-    barrier = pltpu.get_barrier_semaphore()
-    for d in range(1, BLKS):
-        pl.semaphore_signal(barrier, inc=1, device_id=(o, lax.rem(b + d, BLKS)), device_id_type=MESH)
-    pl.semaphore_wait(barrier, BLKS - 1)
-    copies = []
-    for d in (2, 1, 3):
-        to = lax.rem(b + d, BLKS)
-        copy = pltpu.make_async_remote_copy(
-            src_ref=part.at[to], dst_ref=land.at[d - 1], send_sem=send.at[d - 1],
-            recv_sem=recv.at[d - 1], device_id=(o, to), device_id_type=MESH)
-        copy.start()
-        copies.append(copy)
-    for copy in copies:
-        copy.wait_recv()
-    for l in range(LEAVES):
-        total = part[b, l].astype(F32)
-        for d in range(BLKS - 1):
-            total = total + land[d, l].astype(F32)
-        out[:, l, :] = total
-    for copy in copies:
-        copy.wait_send()
-
-
 def on_device(points, charges, leaf_interp, root_interp, skeleton_index, root_index, near_list, far_list, far_count):
-    o = lax.axis_index("leaf").astype(jnp.int32)
-    b = lax.axis_index("blk").astype(jnp.int32)
     own = jnp.transpose(jnp.concatenate([points, charges], axis=0), (1, 0, 2))
     vmem = pl.BlockSpec(memory_space=pltpu.VMEM)
     smem = pl.BlockSpec(memory_space=pltpu.SMEM)
     hbm = pl.BlockSpec(memory_space=pl.ANY)
     dma = pltpu.SemaphoreType.DMA
 
-    near, skel, fs, wl, wr, root, rts = pl.pallas_call(
-        exchange_kernel,
-        out_shape=(
-            jax.ShapeDtypeStruct((LEAVES, RHS, BLKS * PTS), F32),
-            jax.ShapeDtypeStruct((LEAVES, ROWS, SKEL), BF16),
-            jax.ShapeDtypeStruct((32, 128, 128), BF16),
-            jax.ShapeDtypeStruct((64, RHS, 128), BF16),
-            jax.ShapeDtypeStruct((64, RHS, 128), BF16),
-            jax.ShapeDtypeStruct((32, ROWS, 128), BF16),
-            jax.ShapeDtypeStruct((SKEL, 128), BF16),
-        ),
-        in_specs=[vmem, smem, vmem, vmem, hbm, hbm],
-        out_specs=(vmem,) * 7,
+    out = pl.pallas_call(
+        potential_kernel,
+        out_shape=jax.ShapeDtypeStruct((LEAVES, RHS, PTS), F32),
+        in_specs=[vmem, smem, smem, vmem, vmem, vmem, hbm, hbm],
+        out_specs=vmem,
         scratch_shapes=[
             pltpu.VMEM((BLKS, LEAVES, ROWS, PTS), BF16),
             pltpu.VMEM((2, HALO, RAW, PTS), BF16),
@@ -516,48 +506,29 @@
             pltpu.VMEM((8, ROWS, 128), BF16),
             pltpu.VMEM((4, 8, ROWS, 128), BF16),
             pltpu.VMEM((4, 8, ROWS, 128), BF16),
+            pltpu.VMEM((LEAVES, RHS, BLKS * PTS), F32),
+            pltpu.VMEM((LEAVES, ROWS, SKEL), BF16),
+            pltpu.VMEM((64, 64, 128), BF16),
+            pltpu.VMEM((64, RHS, 128), F32),
+            pltpu.VMEM((64, RHS, 128), F32),
+            pltpu.VMEM((SKEL, 128), BF16),
+            pltpu.VMEM((PAIRS * 128, 128), BF16),
+            pltpu.VMEM((RHS, PAIRS * 128), F32),
+            pltpu.VMEM((LEAVES, PAIRS * 128), F32),
+            pltpu.VMEM((LEAVES, RHS, SKEL), F32),
+            pltpu.VMEM((BLKS, LEAVES, RHS, PTS), BF16),
+            pltpu.VMEM((BLKS - 1, LEAVES, RHS, PTS), BF16),
             dma, dma,
             dma((CHUNKS, 2)), dma((CHUNKS, 2)), dma((CHUNKS, 2)), dma((CHUNKS, 2)),
             dma((2,)), dma((2,)),
             dma((CHUNKS, 4)), dma((CHUNKS, 4)),
             dma((7,)), dma((7,)), dma((3,)), dma((3,)), dma((4,)), dma((4,)),
+            dma((CHUNKS, 3)), dma((CHUNKS, 3)),
         ],
         compiler_params=pltpu.CompilerParams(
             collective_id=0, has_side_effects=True, vmem_limit_bytes=VMEM_LIMIT),
-    )(own, near_list, skeleton_index, root_index, leaf_interp, root_interp)
-
-    source_owner = far_list // LEAVES
-    offset = source_owner - o
-    table = (offset + 2 - (offset > 0).astype(jnp.int32)) * LEAVES + far_list - source_owner * LEAVES
-    live = jnp.arange(FAR, dtype=jnp.int32)[None, :] < far_count[:, None]
-    table = jnp.clip(jnp.where(live, table, table[:, :1]), 0, 63)
-    place = jnp.stack([o, b])
-
-    part = pl.pallas_call(
-        field_kernel,
-        out_shape=jax.ShapeDtypeStruct((BLKS, LEAVES, RHS, PTS), BF16),
-        in_specs=[smem, smem, smem, vmem, vmem, vmem, vmem, vmem, vmem, vmem, hbm, hbm],
-        out_specs=vmem,
-        scratch_shapes=[
-            pltpu.VMEM((LEAVES, SKEL, BLKS * PTS), BF16),
-            pltpu.VMEM((LEAVES, SKEL, SKEL), BF16),
-            dma, dma,
-        ],
-        compiler_params=pltpu.CompilerParams(vmem_limit_bytes=VMEM_LIMIT),
-    )(place, table, far_count, near, skel, fs.reshape(64, 64, 128), wl, wr, root, rts, leaf_interp, root_interp)
-
-    return pl.pallas_call(
-        scatter_kernel,
-        out_shape=jax.ShapeDtypeStruct((RHS, LEAVES, PTS), F32),
-        in_specs=[vmem],
-        out_specs=vmem,
-        scratch_shapes=[
-            pltpu.VMEM((BLKS - 1, LEAVES, RHS, PTS), BF16),
-            dma((BLKS - 1,)), dma((BLKS - 1,)),
-        ],
-        compiler_params=pltpu.CompilerParams(
-            collective_id=1, has_side_effects=True, vmem_limit_bytes=VMEM_LIMIT),
-    )(part)
+    )(own, near_list, far_list, far_list, skeleton_index, root_index, leaf_interp, root_interp)
+    return jnp.transpose(out, (1, 0, 2))
 
 
 def solution(mesh):

time: 100 us -> 62.4 us (0.62)
  the two profiles are of different devices: /device:TPU:68 before, /device:TPU:32 now
where the time goes in v2:
time: 62.4 us; the launch traced here: 62.2 us
  Pallas kernels  58 us (93%)
  local copies, waits for them, and re-layouts  3.48 us (6%)
  other arithmetic  0.73 us (1%)
    pallas_call x1, Pallas kernels, on_device(): pl.pallas_call(potential_kernel, out_shape=jax.ShapeDtypeStruct((LEAVES,...  58 us
    unnamed x2, local copies, waits for them, and re-layouts  1.88 us
    transpose x1, local copies, waits for them, and re-layouts, on_device(): return jnp.transpose(out, (1, 0, 2))  1.6 us

profile of v2, /device:TPU:32, one launch (start us, length us, event | category | flops | bytes accessed | tf_op | source)
XLA Modules:
  0.0 62.2 jit_solution(13101652044882897416)
XLA Ops:
  0.0 0.9 %copy.10 = bf16[16,16,128]{2,0,1:T(8,128)(2,1)S(1)} copy(bf16[16,16,128]{2,1,0:T(8,128)(2,1)} %param.10) | data formatting | bytes 131072 | tf_op args[1]
  0.9 1.0 %copy.9 = bf16[64,16,128]{2,0,1:T(8,128)(2,1)S(1)} copy(bf16[64,16,128]{2,1,0:T(8,128)(2,1)} %param.9) | data formatting | bytes 524288 | tf_op args[0]
  1.9 0.7 %maximum_bitcast_fusion.own = bf16[16,80,128]{2,1,0:T(8,128)(2,1)} fusion(bf16[16,16,128]{2,0,1:T(8,128)(2,1)S(1)} %copy.10, bf16[64,16,128]{2,0,1:T(8,128)(2,1)S(1)} %copy.9), kind=kLoop, calls=%fused_computation | loop fusion | flops 655360 | bytes 655360 | tf_op jit(solution)/shard_map/transpose | solution.py:488
  2.6 58.0 %shard_map.82 = f32[16,16,128]{2,1,0:T(8,128)} custom-call(bf16[16,80,128]{2,1,0:T(8,128)(2,1)} %maximum_bitcast_fusion.own, s32[16,10]{1,0:T(8,128)} %nl.1, s32[16,32]{1,0:T(8,128)} %fl_v.1, s32[16,32]{1,0:T(8,128)} %fl_v.1, s32[16,256]{1,0:T(8,128)} %si.1, s32[1,256]{1,0:T(1,128)} %ri.1, bf16[16,256,512]{2,1,0:T(8,128)(2,1)} %li_hbm.1, ...), custom_call_target="tpu_custom_call" | custom-call | tf_op jit(solution)/shard_map/pallas_call | solution.py:494
  60.6 1.6 %copy.11 = f32[16,16,128]{2,1,0:T(8,128)} copy(f32[16,16,128]{2,0,1:T(8,128)} %bitcast.3) | data formatting | bytes 262144 | tf_op jit(solution)/shard_map/transpose | solution.py:531

commit v3 on v2

--- a/solution.py
+++ b/solution.py
@@ -24,7 +24,7 @@
 OWNERS = 64
 CHUNKS = 4
 CHUNK = LEAVES // CHUNKS
-AHEAD = 2
+AHEAD = 3
 STEPS = (-2, -1, 1, 2)
 PAIRS = FAR // 2
 VMEM_LIMIT = 58 * 2**20
@@ -57,12 +57,12 @@
 
 
 def potential_kernel(
-    own, nl, fl_s, fl_v, si, ri, li_hbm, rt_hbm,
+    points, charges, nl, fl_s, fl_v, si, ri, li_hbm, rt_hbm,
     out,
-    gath, halo, srow, swgt, li, rt, fout, fin, rbuf,
-    near_o, skel_o, fs, wl, wr, rts, sall, wall, mask, farsum, part, land,
+    own, gath, halo, srow, swgt, li, rt, fout, fin, rbuf,
+    near_o, skel_o, fs, wl, wr, rts, sall, wall, mask, farsum, part, land, rfs,
     li_sem, rt_sem, y_send, y_recv, f_send, f_recv, h_send, h_recv,
-    far_send, far_recv, z_send, z_recv, x_send, x_recv, c_send, c_recv, s_send, s_recv,
+    far_send, far_recv, z_send, z_recv, x_send, x_recv, c_send, c_recv, s_send, s_recv, r_send, r_recv,
 ):
     o = lax.axis_index("leaf")
     b = lax.axis_index("blk")
@@ -97,6 +97,23 @@
         @pl.when((o + step >= 0) & (o + step < OWNERS))
         def _():
             greet(o + step, b)
+
+    for h in range(2):
+        for g in range(DIM // 16):
+            v = points[g * 16:(g + 1) * 16, h * 8:(h + 1) * 8, :].astype(F32)
+            own[h * 8:(h + 1) * 8, g * 16:(g + 1) * 16, :] = jnp.swapaxes(v, 0, 1).astype(BF16)
+        v = charges[:, h * 8:(h + 1) * 8, :].astype(F32)
+        own[h * 8:(h + 1) * 8, DIM:RAW, :] = jnp.swapaxes(v, 0, 1).astype(BF16)
+
+    @pl.loop(0, LEAVES, unroll=2)
+    def _(l):
+        raw = own[l]
+        aug = aug_rows(raw[:DIM])
+        gath[b, l, 0:RAW, :] = raw
+        gath[b, l, RAW:ROWS, :] = aug
+        srow[HALO + l] = to_rows(raw[:DIM], aug)
+        swgt[HALO + l] = raw[DIM:]
+
     pl.semaphore_wait(barrier, 14 + jnp.minimum(o, 2) + jnp.minimum(OWNERS - 1 - o, 2))
 
     def remote(src, dst, ssem, rsem, leaf, blk):
@@ -139,15 +156,6 @@
         ref = gath.at[src, part, pl.ds(0, RAW)]
         return remote(ref, ref, f_send.at[c, k], f_recv.at[c, k], o, to)
 
-    @pl.loop(0, LEAVES)
-    def _(l):
-        raw = own[l]
-        aug = aug_rows(raw[:DIM])
-        gath[b, l, 0:RAW, :] = raw
-        gath[b, l, RAW:ROWS, :] = aug
-        srow[HALO + l] = to_rows(raw[:DIM], aug)
-        swgt[HALO + l] = raw[DIM:]
-
     def take_halo(side, at):
         @pl.loop(0, HALO)
         def _(l):
@@ -191,7 +199,7 @@
         near_o[l] = jnp.dot(w, p, preferred_element_type=F32)
 
     def near_range(lo, hi):
-        @pl.loop(lo, hi)
+        @pl.loop(lo, hi, unroll=2)
         def _(l):
             near_leaf(l)
 
@@ -263,23 +271,21 @@
             direct[c + AHEAD][1].start()
         if c > 0:
             chunk_work(c - 1)
-            near_range((c - 1) * CHUNK, (c - 1) * CHUNK + 2)
+            near_range((c - 1) * CHUNK, c * CHUNK)
     chunk_work(CHUNKS - 1)
 
     rt_copy.wait()
     ridx = ri[0:1, :]
-    s_id = lax.broadcasted_iota(jnp.int32, (SKEL, SKEL), 0)
-
-    def root_step(l, carry):
-        pts, wgt = carry
-        hot = jnp.where(s_id + l * SKEL == ridx, 1.0, 0.0).astype(BF16)
-        pts = pts + jnp.dot(skel_o[l], hot, preferred_element_type=F32)
-        rows = rt[l, pl.ds(pl.multiple_of(half * 128, 128), 128), :]
-        wgt = wgt + lax.dot_general(skel_o[l, DIM:RAW, :], rows, NT, preferred_element_type=F32)
-        return pts, wgt
-
-    pts, wgt = lax.fori_loop(
-        0, LEAVES, root_step, (jnp.zeros((ROWS, SKEL), F32), jnp.zeros((RHS, 128), F32)))
+    s_id = lax.broadcasted_iota(jnp.int32, (4 * SKEL, SKEL), 0)
+    pts = jnp.zeros((ROWS, SKEL), F32)
+    wgt = jnp.zeros((RHS, 128), F32)
+    rows = pl.ds(pl.multiple_of(half * 128, 128), 128)
+    for l in range(0, LEAVES, 4):
+        hot = jnp.where(s_id == ridx - l * SKEL, 1.0, 0.0).astype(BF16)
+        four = jnp.concatenate([skel_o[l + e] for e in range(4)], axis=1)
+        lift = jnp.concatenate([rt[l + e, rows, :] for e in range(4)], axis=1)
+        pts = pts + jnp.dot(four, hot, preferred_element_type=F32)
+        wgt = wgt + lax.dot_general(four[DIM:RAW], lift, NT, preferred_element_type=F32)
     mine = jnp.where(half == 0, pts[:, :128], pts[:, 128:])
 
     @pl.when(sender)
@@ -318,18 +324,6 @@
     for h in range(2):
         v = pts[:, h * 128:(h + 1) * 128]
         rts[h * 128:(h + 1) * 128, :] = to_rows(v[:DIM], v[RAW:])
-
-    near_range(2, 4)
-    near_range(6, 8)
-    near_range(10, 12)
-
-    @pl.when(sender)
-    def _():
-        for d in range(1, 8):
-            root_z_wait(d).wait_recv()
-        for d in range(1, 4):
-            root_x(d).start()
-        root_c(0).start()
 
     near_range(12, 16)
 
@@ -394,7 +388,15 @@
             farsum[l] = jnp.dot(w0, p[:, :SKEL], preferred_element_type=F32)
             farsum[l + 1] = jnp.dot(w1, p[:, SKEL:], preferred_element_type=F32)
 
-    far_range(0, 6)
+    @pl.when(sender)
+    def _():
+        for d in range(1, 8):
+            root_z_wait(d).wait_recv()
+        for d in range(1, 4):
+            root_x(d).start()
+        root_c(0).start()
+
+    far_range(0, 10)
 
     @pl.when(sender)
     def _():
@@ -402,7 +404,21 @@
             root_x_wait(d).wait_recv()
             root_c(d).start()
 
-    far_range(6, 16)
+    far_range(10, 16)
+
+    def scatter_copy(c, d):
+        to = lax.rem(b + d, BLKS)
+        return remote(part.at[to, leaves(c)], land.at[d - 1, leaves(c)],
+                      s_send.at[c, d - 1], s_recv.at[c, d - 1], o, to)
+
+    for c in range(CHUNKS):
+        for l in range(c * CHUNK, (c + 1) * CHUNK):
+            total = near_o[l] + jnp.dot(farsum[l].astype(BF16), li[l], preferred_element_type=F32)
+            total = total.astype(BF16)
+            for d in range(BLKS):
+                part[d, l] = total[:, d * 128:(d + 1) * 128]
+        for d in (2, 1, 3):
+            scatter_copy(c, d).start()
 
     @pl.when(jnp.logical_not(sender))
     def _():
@@ -428,29 +444,28 @@
 
     rf = lax.fori_loop(0, 8, root_group, jnp.zeros((RHS, SKEL), F32), unroll=2).astype(BF16)
 
-    def scatter_copy(c, d):
-        to = lax.rem(b + d, BLKS)
-        return remote(part.at[to, leaves(c)], land.at[d - 1, leaves(c)],
-                      s_send.at[c, d - 1], s_recv.at[c, d - 1], o, to)
-
+    rfs[b] = rf
+
+    def root_sum(d):
+        return remote(rfs.at[b], rfs.at[b], r_send.at[d - 1], r_recv.at[d - 1], o, lax.rem(b + d, BLKS))
+
+    for d in range(1, BLKS):
+        root_sum(d).start()
+    for d in range(1, BLKS):
+        root_sum(d).wait_recv()
+    field = rfs[0].astype(F32)
+    for d in range(1, BLKS):
+        field = field + rfs[d].astype(F32)
+    field = field.astype(BF16)
+    mine = pl.ds(pl.multiple_of(b * 128, 128), 128)
     for c in range(CHUNKS):
         group = range(c * CHUNK, (c + 1) * CHUNK)
-        fields = [
-            (farsum[l] + jnp.dot(rf, rt[l], preferred_element_type=F32)).astype(BF16) for l in group
-        ]
-        for l, field in zip(group, fields):
-            total = near_o[l] + jnp.dot(field, li[l], preferred_element_type=F32)
-            total = total.astype(BF16)
-            for d in range(BLKS):
-                part[d, l] = total[:, d * 128:(d + 1) * 128]
-        for d in (2, 1, 3):
-            scatter_copy(c, d).start()
-
-    for c in range(CHUNKS):
-        for d in (1, 2, 3):
+        lifted = [jnp.dot(field, rt[l], preferred_element_type=F32).astype(BF16) for l in group]
+        for d in range(1, BLKS):
             scatter_copy(c, d).wait_recv()
-        for l in range(c * CHUNK, (c + 1) * CHUNK):
-            total = part[b, l].astype(F32)
+        for l, v in zip(group, lifted):
+            total = jnp.dot(v, li[l, :, mine], preferred_element_type=F32)
+            total = total + part[b, l].astype(F32)
             for d in range(BLKS - 1):
                 total = total + land[d, l].astype(F32)
             out[l] = total
@@ -474,6 +489,9 @@
             direct[c][k].wait_send()
             forward(c, k).wait_send()
 
+    for d in range(1, BLKS):
+        root_sum(d).wait_send()
+
     @pl.when(sender)
     def _():
         for d in range(1, 8):
@@ -485,7 +503,6 @@
 
 
 def on_device(points, charges, leaf_interp, root_interp, skeleton_index, root_index, near_list, far_list, far_count):
-    own = jnp.transpose(jnp.concatenate([points, charges], axis=0), (1, 0, 2))
     vmem = pl.BlockSpec(memory_space=pltpu.VMEM)
     smem = pl.BlockSpec(memory_space=pltpu.SMEM)
     hbm = pl.BlockSpec(memory_space=pl.ANY)
@@ -494,9 +511,10 @@
     out = pl.pallas_call(
         potential_kernel,
         out_shape=jax.ShapeDtypeStruct((LEAVES, RHS, PTS), F32),
-        in_specs=[vmem, smem, smem, vmem, vmem, vmem, hbm, hbm],
+        in_specs=[vmem, vmem, smem, smem, vmem, vmem, vmem, hbm, hbm],
         out_specs=vmem,
         scratch_shapes=[
+            pltpu.VMEM((LEAVES, RAW, PTS), BF16),
             pltpu.VMEM((BLKS, LEAVES, ROWS, PTS), BF16),
             pltpu.VMEM((2, HALO, RAW, PTS), BF16),
             pltpu.VMEM((2 * HALO + LEAVES, 128, 128), BF16),
@@ -518,16 +536,17 @@
             pltpu.VMEM((LEAVES, RHS, SKEL), F32),
             pltpu.VMEM((BLKS, LEAVES, RHS, PTS), BF16),
             pltpu.VMEM((BLKS - 1, LEAVES, RHS, PTS), BF16),
+            pltpu.VMEM((BLKS, RHS, SKEL), BF16),
             dma, dma,
             dma((CHUNKS, 2)), dma((CHUNKS, 2)), dma((CHUNKS, 2)), dma((CHUNKS, 2)),
             dma((2,)), dma((2,)),
             dma((CHUNKS, 4)), dma((CHUNKS, 4)),
             dma((7,)), dma((7,)), dma((3,)), dma((3,)), dma((4,)), dma((4,)),
-            dma((CHUNKS, 3)), dma((CHUNKS, 3)),
+            dma((CHUNKS, 3)), dma((CHUNKS, 3)), dma((3,)), dma((3,)),
         ],
         compiler_params=pltpu.CompilerParams(
             collective_id=0, has_side_effects=True, vmem_limit_bytes=VMEM_LIMIT),
-    )(own, near_list, far_list, far_list, skeleton_index, root_index, leaf_interp, root_interp)
+    )(points, charges, near_list, far_list, far_list, skeleton_index, root_index, leaf_interp, root_interp)
     return jnp.transpose(out, (1, 0, 2))
 
 

time: 62.4 us -> 58.4 us (0.936)
  the two profiles are of different devices: /device:TPU:32 before, /device:TPU:1 now
where the time goes in v3:
time: 58.4 us; the launch traced here: 58.3 us
  Pallas kernels  56.7 us (97%)
  local copies, waits for them, and re-layouts  1.6 us (3%)
    pallas_call x1, Pallas kernels, on_device(): pl.pallas_call(potential_kernel, out_shape=jax.ShapeDtypeStruct((LEAVES,...  56.7 us
    transpose x1, local copies, waits for them, and re-layouts, on_device(): return jnp.transpose(out, (1, 0, 2))  1.6 us

profile of v3, /device:TPU:1, one launch (start us, length us, event | category | flops | bytes accessed | tf_op | source)
XLA Modules:
  0.0 58.3 jit_solution(4920699706623321164)
XLA Ops:
  0.0 56.7 %shard_map.82 = f32[16,16,128]{2,1,0:T(8,128)} custom-call(bf16[64,16,128]{2,1,0:T(8,128)(2,1)} %points.1, bf16[16,16,128]{2,1,0:T(8,128)(2,1)} %charges.1, s32[16,10]{1,0:T(8,128)} %nl.1, s32[16,32]{1,0:T(8,128)} %fl_v.1, s32[16,32]{1,0:T(8,128)} %fl_v.1, s32[16,256]{1,0:T(8,128)} %si.1, s32[1,256]{1,0:T(1,128)} %ri.1, bf16[16,256,512]{2,1,0:T(8,128)(2,1)} %li_hbm.1, ...), custom_call_target="tpu_custom_call" | custom-call | tf_op jit(solution)/shard_map/pallas_call | solution.py:511
  56.7 1.6 %copy.9 = f32[16,16,128]{2,1,0:T(8,128)} copy(f32[16,16,128]{2,0,1:T(8,128)} %bitcast.1) | data formatting | bytes 262144 | tf_op jit(solution)/shard_map/transpose | solution.py:550

commit v4 on v3

--- a/solution.py
+++ b/solution.py
@@ -22,11 +22,14 @@
 NEAR = 10
 FAR = 32
 OWNERS = 64
-CHUNKS = 4
+CHUNKS = 8
 CHUNK = LEAVES // CHUNKS
-AHEAD = 3
+QUADS = 4
+QUAD = LEAVES // QUADS
 STEPS = (-2, -1, 1, 2)
 PAIRS = FAR // 2
+FAR_A = 10
+FAR_B = 12
 VMEM_LIMIT = 58 * 2**20
 
 
@@ -57,11 +60,11 @@
 
 
 def potential_kernel(
-    points, charges, nl, fl_s, fl_v, si, ri, li_hbm, rt_hbm,
+    points_hbm, charges_hbm, nl, fl_s, fl_v, si, ri, li_hbm, rt_hbm,
     out,
-    own, gath, halo, srow, swgt, li, rt, fout, fin, rbuf,
+    points, charges, own, gath, halo, srow, swgt, li, rt, fout, fin, rbuf,
     near_o, skel_o, fs, wl, wr, rts, sall, wall, mask, farsum, part, land, rfs,
-    li_sem, rt_sem, y_send, y_recv, f_send, f_recv, h_send, h_recv,
+    p_sem, q_sem, li_sem, rt_sem, y_send, y_recv, h_send, h_recv,
     far_send, far_recv, z_send, z_recv, x_send, x_recv, c_send, c_recv, s_send, s_recv, r_send, r_recv,
 ):
     o = lax.axis_index("leaf")
@@ -77,8 +80,10 @@
 
     li_copy = pltpu.make_async_copy(li_hbm, li, li_sem)
     rt_copy = pltpu.make_async_copy(rt_hbm, rt, rt_sem)
-    li_copy.start()
-    rt_copy.start()
+    p_copy = pltpu.make_async_copy(points_hbm, points, p_sem)
+    q_copy = pltpu.make_async_copy(charges_hbm, charges, q_sem)
+    p_copy.start()
+    q_copy.start()
 
     barrier = pltpu.get_barrier_semaphore()
 
@@ -98,6 +103,10 @@
         def _():
             greet(o + step, b)
 
+    p_copy.wait()
+    q_copy.wait()
+    li_copy.start()
+    rt_copy.start()
     for h in range(2):
         for g in range(DIM // 16):
             v = points[g * 16:(g + 1) * 16, h * 8:(h + 1) * 8, :].astype(F32)
@@ -137,24 +146,16 @@
     def leaves(c):
         return pl.ds(c * CHUNK, CHUNK)
 
-    direct = []
+    def gather_copy(c, d):
+        return remote(own.at[leaves(c)], gath.at[b, leaves(c), pl.ds(0, RAW)],
+                      y_send.at[c, d - 1], y_recv.at[c, d - 1], o, lax.rem(b + d, BLKS))
+
+    def leaves(c):
+        return pl.ds(c * CHUNK, CHUNK)
+
     for c in range(CHUNKS):
-        pair = []
-        for k, to in enumerate((up, down)):
-            pair.append(remote(
-                own.at[leaves(c)], gath.at[b, leaves(c), pl.ds(0, RAW)],
-                y_send.at[c, k], y_recv.at[c, k], o, to))
-        direct.append(pair)
-        if c < AHEAD:
-            pair[0].start()
-            pair[1].start()
-
-    def forward(c, k):
-        src = (down, up)[k]
-        to = (up, down)[k]
-        part = pl.ds(c * CHUNK + k * (CHUNK // 2), CHUNK // 2)
-        ref = gath.at[src, part, pl.ds(0, RAW)]
-        return remote(ref, ref, f_send.at[c, k], f_recv.at[c, k], o, to)
+        for d in (2, 1, 3):
+            gather_copy(c, d).start()
 
     def take_halo(side, at):
         @pl.loop(0, HALO)
@@ -168,24 +169,6 @@
         def _(l):
             srow[at + l] = jnp.zeros((128, 128), BF16)
             swgt[at + l] = jnp.zeros((RHS, 128), BF16)
-
-    @pl.when(has_low)
-    def _():
-        h_up.wait_recv()
-        take_halo(0, 0)
-
-    @pl.when(jnp.logical_not(has_low))
-    def _():
-        no_halo(0)
-
-    @pl.when(has_high)
-    def _():
-        h_down.wait_recv()
-        take_halo(1, HALO + LEAVES)
-
-    @pl.when(jnp.logical_not(has_high))
-    def _():
-        no_halo(HALO + LEAVES)
 
     near_base = HALO - o * LEAVES
 
@@ -198,10 +181,10 @@
         p = jnp.exp(x).astype(BF16)
         near_o[l] = jnp.dot(w, p, preferred_element_type=F32)
 
-    def near_range(lo, hi):
-        @pl.loop(lo, hi, unroll=2)
-        def _(l):
-            near_leaf(l)
+    def near_chunk(c):
+        @pl.loop(0, CHUNK, unroll=2)
+        def _(i):
+            near_leaf(c * CHUNK + i)
 
     def skeleton_leaf(l):
         t = jnp.concatenate([gath[k, l] for k in range(BLKS)], axis=1)
@@ -226,52 +209,65 @@
         fout[q] = jnp.where(lane < 64, a, c).astype(BF16)
 
     def far_copy(c, k):
-        part = pl.ds(c * 2, 2)
+        part = pl.ds(c * (CHUNK // 2), CHUNK // 2)
         return remote(fout.at[part], fin.at[3 - k, part], far_send.at[c, k], far_recv.at[c, 3 - k],
                       o + STEPS[k], b)
 
     def far_wait(c, k):
-        part = pl.ds(c * 2, 2)
+        part = pl.ds(c * (CHUNK // 2), CHUNK // 2)
         return remote(fout.at[part], fin.at[k, part], far_send.at[c, k], far_recv.at[c, k],
                       o + STEPS[k], b)
 
-    li_copy.wait()
     opp = lax.rem(b + 2, BLKS)
 
     def chunk_work(c):
-        @pl.loop(c * CHUNK, (c + 1) * CHUNK)
-        def _(l):
+        for d in (2, 1, 3):
+            gather_copy(c, d).wait_recv()
+
+        @pl.loop(0, CHUNK, unroll=2)
+        def _(i):
+            l = c * CHUNK + i
             gath[up, l, RAW:ROWS, :] = aug_rows(gath[up, l, 0:DIM, :])
             gath[down, l, RAW:ROWS, :] = aug_rows(gath[down, l, 0:DIM, :])
-
-        forward(c, 0).wait_recv()
-        forward(c, 1).wait_recv()
-
-        @pl.loop(c * CHUNK, (c + 1) * CHUNK, unroll=2)
-        def _(l):
             gath[opp, l, RAW:ROWS, :] = aug_rows(gath[opp, l, 0:DIM, :])
             skeleton_leaf(l)
 
-        @pl.loop(c * 2, c * 2 + 2)
-        def _(q):
-            far_pair(q)
+        @pl.loop(0, CHUNK // 2)
+        def _(i):
+            far_pair(c * (CHUNK // 2) + i)
 
         for k, step in enumerate(STEPS):
             @pl.when((o + step >= 0) & (o + step < OWNERS))
             def _():
                 far_copy(c, k).start()
 
-    for c in range(CHUNKS):
-        direct[c][0].wait_recv()
-        forward(c, 0).start()
-        direct[c][1].wait_recv()
-        forward(c, 1).start()
-        if c + AHEAD < CHUNKS:
-            direct[c + AHEAD][0].start()
-            direct[c + AHEAD][1].start()
-        if c > 0:
-            chunk_work(c - 1)
-            near_range((c - 1) * CHUNK, c * CHUNK)
+    def halo_rows():
+        @pl.when(has_low)
+        def _():
+            h_up.wait_recv()
+            take_halo(0, 0)
+
+        @pl.when(jnp.logical_not(has_low))
+        def _():
+            no_halo(0)
+
+        @pl.when(has_high)
+        def _():
+            h_down.wait_recv()
+            take_halo(1, HALO + LEAVES)
+
+        @pl.when(jnp.logical_not(has_high))
+        def _():
+            no_halo(HALO + LEAVES)
+
+    halo_rows()
+    li_copy.wait()
+
+    @pl.loop(0, CHUNKS - 1)
+    def _(c):
+        chunk_work(c)
+        near_chunk(c)
+
     chunk_work(CHUNKS - 1)
 
     rt_copy.wait()
@@ -325,7 +321,7 @@
         v = pts[:, h * 128:(h + 1) * 128]
         rts[h * 128:(h + 1) * 128, :] = to_rows(v[:DIM], v[RAW:])
 
-    near_range(12, 16)
+    near_chunk(CHUNKS - 1)
 
     wlane = lax.broadcasted_iota(jnp.int32, (RHS, 128), 1)
     for k, step in enumerate(STEPS):
@@ -396,29 +392,30 @@
             root_x(d).start()
         root_c(0).start()
 
-    far_range(0, 10)
-
-    @pl.when(sender)
-    def _():
-        for d in range(1, 4):
-            root_x_wait(d).wait_recv()
-            root_c(d).start()
-
-    far_range(10, 16)
-
     def scatter_copy(c, d):
         to = lax.rem(b + d, BLKS)
-        return remote(part.at[to, leaves(c)], land.at[d - 1, leaves(c)],
+        return remote(part.at[to, pl.ds(c * QUAD, QUAD)], land.at[d - 1, pl.ds(c * QUAD, QUAD)],
                       s_send.at[c, d - 1], s_recv.at[c, d - 1], o, to)
 
-    for c in range(CHUNKS):
-        for l in range(c * CHUNK, (c + 1) * CHUNK):
+    def far_down(c):
+        for l in range(c * QUAD, (c + 1) * QUAD):
             total = near_o[l] + jnp.dot(farsum[l].astype(BF16), li[l], preferred_element_type=F32)
             total = total.astype(BF16)
             for d in range(BLKS):
                 part[d, l] = total[:, d * 128:(d + 1) * 128]
         for d in (2, 1, 3):
             scatter_copy(c, d).start()
+
+    far_range(0, FAR_A)
+    @pl.when(sender)
+    def _():
+        for d in range(1, 4):
+            root_x_wait(d).wait_recv()
+            root_c(d).start()
+
+    far_range(FAR_A, FAR_B)
+    for c in range(FAR_B // QUAD):
+        far_down(c)
 
     @pl.when(jnp.logical_not(sender))
     def _():
@@ -451,6 +448,10 @@
 
     for d in range(1, BLKS):
         root_sum(d).start()
+    far_range(FAR_B, LEAVES)
+    for c in range(FAR_B // QUAD, QUADS):
+        far_down(c)
+
     for d in range(1, BLKS):
         root_sum(d).wait_recv()
     field = rfs[0].astype(F32)
@@ -458,8 +459,8 @@
         field = field + rfs[d].astype(F32)
     field = field.astype(BF16)
     mine = pl.ds(pl.multiple_of(b * 128, 128), 128)
-    for c in range(CHUNKS):
-        group = range(c * CHUNK, (c + 1) * CHUNK)
+    for c in range(QUADS):
+        group = range(c * QUAD, (c + 1) * QUAD)
         lifted = [jnp.dot(field, rt[l], preferred_element_type=F32).astype(BF16) for l in group]
         for d in range(1, BLKS):
             scatter_copy(c, d).wait_recv()
@@ -484,13 +485,12 @@
             def _():
                 far_copy(c, k).wait_send()
         for d in (1, 2, 3):
-            scatter_copy(c, d).wait_send()
-        for k in range(2):
-            direct[c][k].wait_send()
-            forward(c, k).wait_send()
+            gather_copy(c, d).wait_send()
 
     for d in range(1, BLKS):
         root_sum(d).wait_send()
+        for c in range(QUADS):
+            scatter_copy(c, d).wait_send()
 
     @pl.when(sender)
     def _():
@@ -511,9 +511,11 @@
     out = pl.pallas_call(
         potential_kernel,
         out_shape=jax.ShapeDtypeStruct((LEAVES, RHS, PTS), F32),
-        in_specs=[vmem, vmem, smem, smem, vmem, vmem, vmem, hbm, hbm],
+        in_specs=[hbm, hbm, smem, smem, vmem, vmem, vmem, hbm, hbm],
         out_specs=vmem,
         scratch_shapes=[
+            pltpu.VMEM((DIM, LEAVES, PTS), BF16),
+            pltpu.VMEM((RHS, LEAVES, PTS), BF16),
             pltpu.VMEM((LEAVES, RAW, PTS), BF16),
             pltpu.VMEM((BLKS, LEAVES, ROWS, PTS), BF16),
             pltpu.VMEM((2, HALO, RAW, PTS), BF16),
@@ -537,12 +539,12 @@
             pltpu.VMEM((BLKS, LEAVES, RHS, PTS), BF16),
             pltpu.VMEM((BLKS - 1, LEAVES, RHS, PTS), BF16),
             pltpu.VMEM((BLKS, RHS, SKEL), BF16),
-            dma, dma,
-            dma((CHUNKS, 2)), dma((CHUNKS, 2)), dma((CHUNKS, 2)), dma((CHUNKS, 2)),
+            dma, dma, dma, dma,
+            dma((CHUNKS, 3)), dma((CHUNKS, 3)),
             dma((2,)), dma((2,)),
             dma((CHUNKS, 4)), dma((CHUNKS, 4)),
             dma((7,)), dma((7,)), dma((3,)), dma((3,)), dma((4,)), dma((4,)),
-            dma((CHUNKS, 3)), dma((CHUNKS, 3)), dma((3,)), dma((3,)),
+            dma((QUADS, 3)), dma((QUADS, 3)), dma((3,)), dma((3,)),
         ],
         compiler_params=pltpu.CompilerParams(
             collective_id=0, has_side_effects=True, vmem_limit_bytes=VMEM_LIMIT),

time: 58.4 us -> 55.7 us (0.954)
  Pallas kernels: 56.7 us -> 53.9 us
    pallas_call x1, Pallas kernels: 56.7 us -> 53.9 us  [on_device(): pl.pallas_call(potential_kernel, out_shape=jax.ShapeDtypeStruct((LEAVES,...]
where the time goes in v4:
time: 55.7 us; the launch traced here: 55.5 us
  Pallas kernels  53.9 us (97%)
  local copies, waits for them, and re-layouts  1.6 us (3%)
    pallas_call x1, Pallas kernels, on_device(): pl.pallas_call(potential_kernel, out_shape=jax.ShapeDtypeStruct((LEAVES,...  53.9 us
    transpose x1, local copies, waits for them, and re-layouts, on_device(): return jnp.transpose(out, (1, 0, 2))  1.6 us

profile of v4, /device:TPU:1, one launch (start us, length us, event | category | flops | bytes accessed | tf_op | source)
XLA Modules:
  0.0 55.5 jit_solution(15683202182837279324)
XLA Ops:
  0.0 53.9 %shard_map.82 = f32[16,16,128]{2,1,0:T(8,128)} custom-call(bf16[64,16,128]{2,1,0:T(8,128)(2,1)} %points_hbm.1, bf16[16,16,128]{2,1,0:T(8,128)(2,1)} %charges_hbm.1, s32[16,10]{1,0:T(8,128)} %nl.1, s32[16,32]{1,0:T(8,128)} %fl_v.1, s32[16,32]{1,0:T(8,128)} %fl_v.1, s32[16,256]{1,0:T(8,128)} %si.1, s32[1,256]{1,0:T(1,128)} %ri.1, ...), custom_call_target="tpu_custom_call" | custom-call | tf_op jit(solution)/shard_map/pallas_call | solution.py:511
  53.9 1.6 %copy.9 = f32[16,16,128]{2,1,0:T(8,128)} copy(f32[16,16,128]{2,0,1:T(8,128)} %bitcast.1) | data formatting | bytes 262144 | tf_op jit(solution)/shard_map/transpose | solution.py:552

commit v5 on v4

--- a/solution.py
+++ b/solution.py
@@ -114,15 +114,6 @@
         v = charges[:, h * 8:(h + 1) * 8, :].astype(F32)
         own[h * 8:(h + 1) * 8, DIM:RAW, :] = jnp.swapaxes(v, 0, 1).astype(BF16)
 
-    @pl.loop(0, LEAVES, unroll=2)
-    def _(l):
-        raw = own[l]
-        aug = aug_rows(raw[:DIM])
-        gath[b, l, 0:RAW, :] = raw
-        gath[b, l, RAW:ROWS, :] = aug
-        srow[HALO + l] = to_rows(raw[:DIM], aug)
-        swgt[HALO + l] = raw[DIM:]
-
     pl.semaphore_wait(barrier, 14 + jnp.minimum(o, 2) + jnp.minimum(OWNERS - 1 - o, 2))
 
     def remote(src, dst, ssem, rsem, leaf, blk):
@@ -158,7 +149,7 @@
             gather_copy(c, d).start()
 
     def take_halo(side, at):
-        @pl.loop(0, HALO)
+        @pl.loop(0, HALO, unroll=8)
         def _(l):
             raw = halo[side, l]
             srow[at + l] = to_rows(raw[:DIM], aug_rows(raw[:DIM]))
@@ -259,6 +250,15 @@
         @pl.when(jnp.logical_not(has_high))
         def _():
             no_halo(HALO + LEAVES)
+
+    @pl.loop(0, LEAVES, unroll=4)
+    def _(l):
+        raw = own[l]
+        aug = aug_rows(raw[:DIM])
+        gath[b, l, 0:RAW, :] = raw
+        gath[b, l, RAW:ROWS, :] = aug
+        srow[HALO + l] = to_rows(raw[:DIM], aug)
+        swgt[HALO + l] = raw[DIM:]
 
     halo_rows()
     li_copy.wait()
@@ -332,7 +332,7 @@
             for c in range(CHUNKS):
                 far_wait(c, k).wait_recv()
 
-            @pl.loop(0, 8)
+            @pl.loop(0, 8, unroll=8)
             def _(q):
                 v = fin[k, q]
                 even = k * 16 + 2 * q
@@ -439,7 +439,7 @@
         w = jnp.concatenate(wgts, axis=1)
         return acc + lax.dot_general(w, pt, NT, preferred_element_type=F32)
 
-    rf = lax.fori_loop(0, 8, root_group, jnp.zeros((RHS, SKEL), F32), unroll=2).astype(BF16)
+    rf = lax.fori_loop(0, 8, root_group, jnp.zeros((RHS, SKEL), F32), unroll=4).astype(BF16)
 
     rfs[b] = rf
 

time: 55.7 us -> 53.9 us (0.968)
  Pallas kernels: 53.9 us -> 52.1 us
    pallas_call x1, Pallas kernels: 53.9 us -> 52.1 us  [on_device(): pl.pallas_call(potential_kernel, out_shape=jax.ShapeDtypeStruct((LEAVES,...]
where the time goes in v5:
time: 53.9 us; the launch traced here: 53.7 us
  Pallas kernels  52.1 us (97%)
  local copies, waits for them, and re-layouts  1.6 us (3%)
    pallas_call x1, Pallas kernels, on_device(): pl.pallas_call(potential_kernel, out_shape=jax.ShapeDtypeStruct((LEAVES,...  52.1 us
    transpose x1, local copies, waits for them, and re-layouts, on_device(): return jnp.transpose(out, (1, 0, 2))  1.6 us

profile of v5, /device:TPU:1, one launch (start us, length us, event | category | flops | bytes accessed | tf_op | source)
XLA Modules:
  0.0 53.7 jit_solution(6460020591615902093)
XLA Ops:
  0.0 52.1 %shard_map.82 = f32[16,16,128]{2,1,0:T(8,128)} custom-call(bf16[64,16,128]{2,1,0:T(8,128)(2,1)} %points_hbm.1, bf16[16,16,128]{2,1,0:T(8,128)(2,1)} %charges_hbm.1, s32[16,10]{1,0:T(8,128)} %nl.1, s32[16,32]{1,0:T(8,128)} %fl_v.1, s32[16,32]{1,0:T(8,128)} %fl_v.1, s32[16,256]{1,0:T(8,128)} %si.1, s32[1,256]{1,0:T(1,128)} %ri.1, ...), custom_call_target="tpu_custom_call" | custom-call | tf_op jit(solution)/shard_map/pallas_call | solution.py:511
  52.1 1.6 %copy.9 = f32[16,16,128]{2,1,0:T(8,128)} copy(f32[16,16,128]{2,0,1:T(8,128)} %bitcast.1) | data formatting | bytes 262144 | tf_op jit(solution)/shard_map/transpose | solution.py:552

commit v6 on v5

--- a/solution.py
+++ b/solution.py
@@ -211,21 +211,21 @@
 
     opp = lax.rem(b + 2, BLKS)
 
-    def chunk_work(c):
+    def chunk_work(c, with_near):
         for d in (2, 1, 3):
             gather_copy(c, d).wait_recv()
 
-        @pl.loop(0, CHUNK, unroll=2)
-        def _(i):
+        for i in range(CHUNK):
             l = c * CHUNK + i
             gath[up, l, RAW:ROWS, :] = aug_rows(gath[up, l, 0:DIM, :])
             gath[down, l, RAW:ROWS, :] = aug_rows(gath[down, l, 0:DIM, :])
             gath[opp, l, RAW:ROWS, :] = aug_rows(gath[opp, l, 0:DIM, :])
             skeleton_leaf(l)
-
-        @pl.loop(0, CHUNK // 2)
-        def _(i):
+        for i in range(CHUNK // 2):
             far_pair(c * (CHUNK // 2) + i)
+        if with_near:
+            for i in range(CHUNK):
+                near_leaf(c * CHUNK + i)
 
         for k, step in enumerate(STEPS):
             @pl.when((o + step >= 0) & (o + step < OWNERS))
@@ -265,10 +265,9 @@
 
     @pl.loop(0, CHUNKS - 1)
     def _(c):
-        chunk_work(c)
-        near_chunk(c)
-
-    chunk_work(CHUNKS - 1)
+        chunk_work(c, True)
+
+    chunk_work(CHUNKS - 1, False)
 
     rt_copy.wait()
     ridx = ri[0:1, :]

time: 53.9 us -> 53.3 us (0.989)
  Pallas kernels: 52.1 us -> 51.5 us
    pallas_call x1, Pallas kernels: 52.1 us -> 51.5 us  [on_device(): pl.pallas_call(potential_kernel, out_shape=jax.ShapeDtypeStruct((LEAVES,...]
where the time goes in v6:
time: 53.3 us; the launch traced here: 53.1 us
  Pallas kernels  51.5 us (97%)
  local copies, waits for them, and re-layouts  1.6 us (3%)
    pallas_call x1, Pallas kernels, on_device(): pl.pallas_call(potential_kernel, out_shape=jax.ShapeDtypeStruct((LEAVES,...  51.5 us
    transpose x1, local copies, waits for them, and re-layouts, on_device(): return jnp.transpose(out, (1, 0, 2))  1.6 us

profile of v6, /device:TPU:1, one launch (start us, length us, event | category | flops | bytes accessed | tf_op | source)
XLA Modules:
  0.0 53.1 jit_solution(8130834012456903957)
XLA Ops:
  0.0 51.5 %shard_map.82 = f32[16,16,128]{2,1,0:T(8,128)} custom-call(bf16[64,16,128]{2,1,0:T(8,128)(2,1)} %points_hbm.1, bf16[16,16,128]{2,1,0:T(8,128)(2,1)} %charges_hbm.1, s32[16,10]{1,0:T(8,128)} %nl.1, s32[16,32]{1,0:T(8,128)} %fl_v.1, s32[16,32]{1,0:T(8,128)} %fl_v.1, s32[16,256]{1,0:T(8,128)} %si.1, s32[1,256]{1,0:T(1,128)} %ri.1, ...), custom_call_target="tpu_custom_call" | custom-call | tf_op jit(solution)/shard_map/pallas_call | solution.py:510
  51.5 1.6 %copy.9 = f32[16,16,128]{2,1,0:T(8,128)} copy(f32[16,16,128]{2,0,1:T(8,128)} %bitcast.1) | data formatting | bytes 262144 | tf_op jit(solution)/shard_map/transpose | solution.py:551

commit v7 on v6

--- a/solution.py
+++ b/solution.py
@@ -438,7 +438,7 @@
         w = jnp.concatenate(wgts, axis=1)
         return acc + lax.dot_general(w, pt, NT, preferred_element_type=F32)
 
-    rf = lax.fori_loop(0, 8, root_group, jnp.zeros((RHS, SKEL), F32), unroll=4).astype(BF16)
+    rf = lax.fori_loop(0, 8, root_group, jnp.zeros((RHS, SKEL), F32), unroll=8).astype(BF16)
 
     rfs[b] = rf
 

time: 53.3 us -> 53.3 us (level)
  no operation moved by 1% of the time
where the time goes in v7:
time: 53.3 us; the launch traced here: 53 us
  Pallas kernels  51.3 us (96%)
  local copies, waits for them, and re-layouts  1.6 us (3%)
    pallas_call x1, Pallas kernels, on_device(): pl.pallas_call(potential_kernel, out_shape=jax.ShapeDtypeStruct((LEAVES,...  51.3 us
    transpose x1, local copies, waits for them, and re-layouts, on_device(): return jnp.transpose(out, (1, 0, 2))  1.6 us

profile of v7, /device:TPU:1, one launch (start us, length us, event | category | flops | bytes accessed | tf_op | source)
XLA Modules:
  0.0 53.0 jit_solution(17995079974648402759)
XLA Ops:
  0.0 51.3 %shard_map.82 = f32[16,16,128]{2,1,0:T(8,128)} custom-call(bf16[64,16,128]{2,1,0:T(8,128)(2,1)} %points_hbm.1, bf16[16,16,128]{2,1,0:T(8,128)(2,1)} %charges_hbm.1, s32[16,10]{1,0:T(8,128)} %nl.1, s32[16,32]{1,0:T(8,128)} %fl_v.1, s32[16,32]{1,0:T(8,128)} %fl_v.1, s32[16,256]{1,0:T(8,128)} %si.1, s32[1,256]{1,0:T(1,128)} %ri.1, ...), custom_call_target="tpu_custom_call" | custom-call | tf_op jit(solution)/shard_map/pallas_call | solution.py:510
  51.4 1.6 %copy.9 = f32[16,16,128]{2,1,0:T(8,128)} copy(f32[16,16,128]{2,0,1:T(8,128)} %bitcast.1) | data formatting | bytes 262144 | tf_op jit(solution)/shard_map/transpose | solution.py:551
